TPU v7x, 32 devices: a whole 2x2x4 slice. The times are simulated.
32 devices in a mesh: parts: 2 (over y), space: 16 (over z, x, core).
Axes of the slice: x: 2, y: 2, z: 4, core: 2. Of those that a mesh axis runs over, the one named last changes fastest.
Arguments:
- grid_latent: bfloat16 [8, 4096, 512], P(None, ('parts', 'space')), parts along dimension 1, may hold values from -6 to 6
- mesh_latent: bfloat16 [8, 1024, 512], P(None, ('parts', 'space')), parts along dimension 1, may hold values from -6 to 6
- send_rows: int32 [32, 16, 2], P(('parts', 'space')), parts along dimension 0, may hold values from 0 to 31
- edge_slot: int32 [3, 4096], P(None, ('parts', 'space')), parts along dimension 1, may hold values from 0 to 63, as said below
- lat_row: int32 [4096], P(('parts', 'space')), parts along dimension 0, may hold values from 0 to 720
- verifying_analyses: float32 [83, 4096], P(None, ('parts', 'space')), parts along dimension 1, may hold values from -6 to 6
- w_send: bfloat16 [512, 512], replicated, may hold values from -0.1875 to 0.1875
- w_recv: bfloat16 [512, 512], replicated, may hold values from -0.1875 to 0.1875
- w_edge: bfloat16 [512, 512], replicated, may hold values from -0.25 to 0.25
- edge_gain: float32 [512], replicated, may hold values from 0.1 to 1.9
- head_matrix: bfloat16 [512, 83], replicated, may hold values from -0.25 to 0.25
Outputs:
- loss: float32 [2], P('parts'), parts along dimension 0
- grad_grid: bfloat16 [8, 4096, 512], P(None, ('parts', 'space')), parts along dimension 1
- grad_mesh: bfloat16 [8, 1024, 512], P(None, ('parts', 'space')), parts along dimension 1
- grad_send: float32 [1024, 512], P('parts'), parts along dimension 0
- grad_recv: float32 [1024, 512], P('parts'), parts along dimension 0
- grad_edge: float32 [1024, 512], P('parts'), parts along dimension 0
- grad_gain: float32 [1024], P('parts'), parts along dimension 0
- head_matrix_sensitivity: float32 [1024, 83], P('parts'), parts along dimension 0
There are 2 independent parts, one for each index of `parts`. A program takes and returns all parts, laid end to end along the dimension named above; an argument that names none is the same for every part. Nothing has to cross between parts.
Inputs may be any that keep to these rules, and one draw needn't show every extreme that they name: `edge_slot`: for a grid point of device q, a value v below 32 names row v of q's own block of mesh nodes; a value 32 + p * 2 + k names the mesh node in row send_rows[p, q, k] of device p's block. The neighbours of one point need not differ.
All inputs are finite; a program needn't handle non-finite values.
Results may differ from a plain program's by a relative error of at most 0.009.
The roundings to bfloat16 on the way count: a program that leaves them out, or rounds other values in their place, can miss the bound.
Values may be sent and summed in bfloat16 or wider, within the bound.
A program may use at most 128 MiB of HBM per device.

v0:
```python
import jax
import jax.numpy as jnp
from jax import lax
from jax.sharding import PartitionSpec as P

LATS = 721


DELTA_SQ = 0.0025
NORM_EPS = 1e-05
PRECISE = lax.Precision.HIGHEST


def softened_absolute(offset):
    return jnp.sqrt(offset * offset + DELTA_SQ)


def smooth_sign_function(offset):
    return offset / jnp.sqrt(offset * offset + DELTA_SQ)


def silu_slope(offset):
    logistic = jax.nn.sigmoid(offset)
    return logistic * (1.0 + offset * (1.0 - logistic))


def project(node_rows, weight):
    return jnp.einsum("mrl,lh->mrh", node_rows, weight, preferred_element_type=jnp.float32).astype(
        jnp.bfloat16
    )


def fold_rows(returned, row_ids, row_count):
    onehot = (row_ids[None, :] == jnp.arange(row_count, dtype=jnp.int32)[:, None]).astype(
        returned.dtype
    )
    return jnp.einsum(
        "rs,msx->mrx", onehot, returned, preferred_element_type=jnp.float32, precision=PRECISE
    )


def body(
    grid_latent,
    mesh_latent,
    send_rows,
    edge_slot,
    lat_row,
    verifying_analyses,
    w_send,
    w_recv,
    w_edge,
    edge_gain,
    head_matrix,
):
    member_outputs = grid_latent.shape[0]
    points = grid_latent.shape[1]
    own_rows = mesh_latent.shape[1]
    peer_count = lax.axis_size("space")
    outgoing = send_rows.reshape(-1)
    arrived = lax.all_to_all(
        jnp.take(mesh_latent, outgoing, axis=1), "space", split_axis=1, concat_axis=1, tiled=True
    )
    gathered = jnp.concatenate([mesh_latent, arrived], axis=1)
    lookup = project(gathered, w_send)
    receiver = jnp.einsum("mgl,lh->mgh", grid_latent, w_recv, preferred_element_type=jnp.float32)
    pre_acts = []
    hidden_acts = []
    normed_list = []
    inv_stds = []
    summed = jnp.zeros(grid_latent.shape, jnp.float32)
    for edge_index in range(edge_slot.shape[0]):
        pre_act = jnp.take(lookup, edge_slot[edge_index], axis=1).astype(jnp.float32) + receiver
        hidden_act = jax.nn.silu(pre_act).astype(jnp.bfloat16)
        edge_out = jnp.einsum("mgh,hl->mgl", hidden_act, w_edge, preferred_element_type=jnp.float32)
        centred = edge_out - jnp.mean(edge_out, axis=-1, keepdims=True)
        inv_std = lax.rsqrt(jnp.mean(centred * centred, axis=-1, keepdims=True) + NORM_EPS)
        normed = centred * inv_std
        summed = summed + normed * edge_gain
        pre_acts.append(pre_act)
        hidden_acts.append(hidden_act)
        normed_list.append(normed)
        inv_stds.append(inv_std)
    refreshed_latent = (grid_latent.astype(jnp.float32) + summed).astype(jnp.bfloat16)
    prognosis_values = jnp.einsum(
        "ozw,wd->odz", refreshed_latent, head_matrix, preferred_element_type=jnp.float32
    )
    lat_weight = jnp.cos(jnp.pi * ((lat_row.astype(jnp.float32) + 0.5) / LATS - 0.5))
    accuracy_term = jnp.mean(softened_absolute(prognosis_values - verifying_analyses[None]), axis=0)
    member_spread = jnp.sum(
        softened_absolute(prognosis_values[:, None] - prognosis_values[None, :]), axis=(0, 1)
    ) / (2.0 * member_outputs * (member_outputs - 1))
    crps_value = accuracy_term - member_spread
    weight_sum, weighted = lax.psum(
        (jnp.sum(lat_weight), jnp.sum(lat_weight * jnp.sum(crps_value, axis=0))), "space"
    )
    dispersion_factor = lat_weight * (points * peer_count / weight_sum)
    couple_derivative = jnp.sum(
        smooth_sign_function(prognosis_values[:, None] - prognosis_values[None, :]), axis=1
    ) / (member_outputs - 1)
    prognosis_sensitivity = (
        dispersion_factor
        * (smooth_sign_function(prognosis_values - verifying_analyses[None]) - couple_derivative)
    ).astype(jnp.bfloat16)
    head_matrix_sensitivity = jnp.einsum(
        "wuj,wru->jr", refreshed_latent, prognosis_sensitivity, preferred_element_type=jnp.float32
    )
    refreshed_latent_adjoint = jnp.einsum(
        "ord,ur->odu", prognosis_sensitivity, head_matrix, preferred_element_type=jnp.float32
    )
    scaled_grad = refreshed_latent_adjoint * edge_gain
    grad_gain = jnp.zeros(edge_gain.shape, jnp.float32)
    grad_edge = jnp.zeros(w_edge.shape, jnp.float32)
    dreceiver = jnp.zeros(receiver.shape, jnp.float32)
    dpre_list = []
    for edge_index in range(edge_slot.shape[0]):
        normed = normed_list[edge_index]
        grad_gain = grad_gain + jnp.sum(refreshed_latent_adjoint * normed, axis=(0, 1))
        dedge = inv_stds[edge_index] * (
            scaled_grad
            - jnp.mean(scaled_grad, axis=-1, keepdims=True)
            - normed * jnp.mean(scaled_grad * normed, axis=-1, keepdims=True)
        )
        dedge = dedge.astype(jnp.bfloat16)
        grad_edge = grad_edge + jnp.einsum(
            "mgh,mgl->hl", hidden_acts[edge_index], dedge, preferred_element_type=jnp.float32
        )
        dhidden = jnp.einsum("mgl,hl->mgh", dedge, w_edge, preferred_element_type=jnp.float32)
        dpre = (dhidden * silu_slope(pre_acts[edge_index])).astype(jnp.bfloat16)
        dreceiver = dreceiver + dpre.astype(jnp.float32)
        dpre_list.append(dpre)
    dreceiver = dreceiver.astype(jnp.bfloat16)
    grad_grid = (
        refreshed_latent_adjoint
        + jnp.einsum("mgh,lh->mgl", dreceiver, w_recv, preferred_element_type=jnp.float32)
    ).astype(jnp.bfloat16)
    grad_recv = jnp.einsum(
        "mgl,mgh->lh", grid_latent, dreceiver, preferred_element_type=jnp.float32
    )
    flat_slots = edge_slot.reshape(-1)
    onehot = (flat_slots[None, :] == jnp.arange(lookup.shape[1], dtype=jnp.int32)[:, None]).astype(
        jnp.bfloat16
    )
    dslot = jnp.einsum(
        "ts,msh->mth",
        onehot,
        jnp.concatenate(dpre_list, axis=1),
        preferred_element_type=jnp.float32,
    ).astype(jnp.bfloat16)
    grad_send = jnp.einsum("mtl,mth->lh", gathered, dslot, preferred_element_type=jnp.float32)
    grad_lat = jnp.einsum("mth,lh->mtl", dslot, w_send, preferred_element_type=jnp.float32)
    returned = lax.all_to_all(
        grad_lat[:, own_rows:].astype(jnp.bfloat16),
        "space",
        split_axis=1,
        concat_axis=1,
        tiled=True,
    ).astype(jnp.float32)
    grad_mesh = grad_lat[:, :own_rows] + fold_rows(returned, outgoing, own_rows)
    totals = lax.psum(
        (grad_send, grad_recv, grad_edge, grad_gain, head_matrix_sensitivity), "space"
    )
    loss_value = (weighted / weight_sum).reshape(1)
    return (
        loss_value,
        grad_grid,
        grad_mesh.astype(jnp.bfloat16),
        totals[0],
        totals[1],
        totals[2],
        totals[3],
        totals[4],
    )


def solution(mesh):
    placed = (
        P(None, ("parts", "space"), None),
        P(None, ("parts", "space"), None),
        P(("parts", "space"), None, None),
        P(None, ("parts", "space")),
        P(("parts", "space")),
        P(None, ("parts", "space")),
        P(),
        P(),
        P(),
        P(),
        P(),
    )
    return jax.shard_map(
        body,
        mesh=mesh,
        in_specs=placed,
        out_specs=(
            P("parts"),
            P(None, ("parts", "space"), None),
            P(None, ("parts", "space"), None),
            P("parts", None),
            P("parts", None),
            P("parts", None),
            P("parts"),
            P("parts", None),
        ),
        check_vma=False,
    )
```

profile of v0, /device:TPU:0, one launch (start us, length us, event | category | flops | bytes accessed | tf_op | source)
XLA Modules:
  0.0 232.0 jit_solution(17858703693512386749)
XLA Ops:
  9.1 2.3 %gather_fusion = bf16[32,8,512]{2,0,1:T(8,128)(2,1)S(1)} fusion(bf16[8,32,512]{2,1,0:T(8,128)(2,1)} %param.14, s32[1024]{0:T(1024)S(1)} %get-tuple-element.92), kind=kCustom, calls=%fused_computation.3 | custom fusion | bytes 524416 | tf_op jit(solution)/shard_map/jit(_take)/gather | solution.py:61
  12.4 7.4 %all-to-all-start = ((bf16[8,32,512]{2,0,1:T(8,128)(2,1)}), bf16[8,32,512]{2,0,1:T(8,128)(2,1)S(1)}, u32[]{:S(2)}, u32[]{:S(2)}) async-start(bf16[8,32,512]{2,0,1:T(8,128)(2,1)} %copy.58), calls=%async_computation | async-start | bytes 524288 | tf_op jit(solution)/shard_map/all_to_all | solution.py:60
  19.9 9.9 %all-to-all-done = bf16[8,32,512]{2,0,1:T(8,128)(2,1)S(1)} async-done(((bf16[8,32,512]{2,0,1:T(8,128)(2,1)}), bf16[8,32,512]{2,0,1:T(8,128)(2,1)S(1)}, u32[]{:S(2)}, u32[]{:S(2)}) %all-to-all-start) | async-done | bytes 262176 | tf_op jit(solution)/shard_map/all_to_all | solution.py:60
  31.4 1.6 gather_fusion.3
  33.1 1.6 gather_fusion.2
  35.4 5.6 %multiply_convert_fusion.6 = (bf16[8,128,512]{2,1,0:T(8,128)(2,1)S(1)}, bf16[8,128,512]{2,1,0:T(8,128)(2,1)S(1)}, bf16[8,128,512]{2,1,0:T(8,128)(2,1)S(1)}, f32[8,128,512]{2,1,0:T(8,128)}) fusion(bf16[128,8,512]{2,1,0:T(8,128)(2,1)} %gather_fusion.3, pred[128]{0:T(512)(128)(4,1)S(1)} %get-tuple-element.63, bf16[128,8,512]{2,1,0:T(8,128)(2,1)} %gather_fusion.2, ...), kind=kOutput, calls=%fused_computation.33 | convolution fusion | flops 549453824 | bytes 9961856 | tf_op jit(solution)/shard_map/mgl,lh->mgh/dot_general | solution.py:65
  48.1 2.9 %fusion.9 = (f32[8,83,128]{2,1,0:T(8,128)}, f32[83,128]{1,0:T(8,128)S(1)}) fusion(f32[8,83,128]{2,0,1:T(8,128)S(1)} %copy.66, f32[8,83,128]{2,1,0:T(8,128)S(1)} %get-tuple-element.87), kind=kLoop, calls=%fused_computation.15 | loop fusion | flops 3984000 | bytes 1062400 | tf_op jit(solution)/shard_map/reduce_sum | solution.py:97
  52.2 31.6 %psum.50 = f32[]{:T(128)} all-reduce(f32[]{:T(128)} %get-tuple-element.54), channel_id=1, replica_groups=mesh['parts'=2,'space'=16] {'space'}, use_global_device_ids=true, to_apply=%region_12.14 | all-reduce | flops 1 | bytes 8 | tf_op jit(solution)/shard_map/psum | solution.py:93
  86.6 2.2 convolution_bitcast_fusion.7
  88.9 4.5 %multiply_reduce_fusion = (f32[512]{0:T(512)S(1)}, f32[8,128]{1,0:T(8,128)S(1)}, f32[8,128]{1,0:T(8,128)S(1)}, f32[512]{0:T(512)S(1)}, f32[8,128]{1,0:T(8,128)S(...) fusion(f32[8,128,512]{2,1,0:T(8,128)S(1)} %get-tuple-element.81, ...), kind=kOutput, calls=%fused_computation.18 | convolution fusion | flops 97511936 | bytes 8692736 | tf_op jit(solution)/shard_map/ord,ur->odu/dot_general | solution.py:107
  93.5 1.8 multiply_convert_fusion.5
  97.3 1.7 multiply_convert_fusion
  99.0 1.7 multiply_convert_fusion.2
  102.4 1.7 multiply_convert_fusion.4
  104.1 1.8 convolution_bitcast_fusion.3
  106.9 1.5 convolution_bitcast_fusion.4
  108.4 1.8 fusion.12
  110.2 1.7 fusion.33
  113.8 3.5 %all-to-all-start.1 = ((bf16[8,32,512]{2,0,1:T(8,128)(2,1)}), bf16[8,32,512]{2,0,1:T(8,128)(2,1)S(1)}, u32[]{:S(2)}, u32[]{:S(2)}) async-start(bf16[8,32,512]{2,0,1:T(8,128)(2,1)} %copy.67), calls=%async_computation.1 | async-start | bytes 524288 | tf_op jit(solution)/shard_map/all_to_all | solution.py:151
  117.4 37.7 %all-reduce = (f32[]{:T(128)}, f32[512]{0:T(512)}) all-reduce(f32[]{:T(128)} %get-tuple-element.55, f32[512]{0:T(512)S(1)} %add_add_fusion), channel_id=1, replica_groups=mesh['parts'=2,'space'=16] {'space'}, use_global_device_ids=true, to_apply=%region_10.12 | all-reduce | flops 513 | bytes 4104 | tf_op jit(solution)/shard_map/psum | solution.py:93
  156.5 3.7 %add_convert_fusion = bf16[8,128,512]{2,1,0:T(8,128)(2,1)} fusion(f32[8,128,512]{2,1,0:T(8,128)S(1)} %copy-done.8, bf16[512,512]{1,0:T(8,128)(2,1)} %param.20, bf16[8,128,512]{2,1,0:T(8,128)(2,1)} %copy-done.25, bf16[8,128,512]{2,1,0:T(8,128)(2,1)} %copy-done.26, bf16[8,128,512]{2,1,0:T(8,128)(2,1)} %copy-done.27), kind=kOutput, calls=%fused_computation.21 | convolution fusion | flops 541065216 | bytes 6815744 | tf_op jit(solution)/shard_map/mgh,lh->mgl/dot_general | solution.py:134
  160.2 2.0 fusion.20
  162.2 56.5 %all-reduce.4.cloned.1.call-done = (f32[512,512]{1,0:T(8,128)}, f32[512,512]{0,1:T(8,128)}, f32[512,512]{1,0:T(8,128)}, f32[512,83]{0,1:T(8,128)}) async-done(((f32[512,512]{1,0:T(8,128)}, f32[512,512]{0,1:T(8,128)}, f32[512,512]{1,0:T(8,128)}, f32[512,83]{0,1:T(8,128)}), (f32[512,512]{1,0:T(8,128)}, f32[512,512]{0,1:T(8,128)}, f32[512,512]{1,0:T(8,128)}, f32[512,83]{0,1:T(8,128)})) %all-reduce.4.cloned.1.call-update) | async-done | bytes 3315728 | tf_op jit(solution)/shard_map/psum | solution.py:159
  218.7 2.7 %copy.73 = f32[512,512]{1,0:T(8,128)} copy(f32[512,512]{0,1:T(8,128)} %get-tuple-element.59) | data formatting | bytes 2097152
  (168 shorter events, 24.5 us)
Async XLA Ops:
  7.2 33.9 %copy-start = (bf16[512,512]{1,0:T(8,128)(2,1)S(1)}, bf16[512,512]{1,0:T(8,128)(2,1)}, u32[]{:S(2)}) copy-start(bf16[512,512]{1,0:T(8,128)(2,1)} %param.21) | copy-start | bytes 1572868
  7.2 12.6 %copy-start.5 = (bf16[8,32,512]{2,1,0:T(8,128)(2,1)S(1)}, bf16[8,32,512]{2,1,0:T(8,128)(2,1)}, u32[]{:S(2)}) copy-start(bf16[8,32,512]{2,1,0:T(8,128)(2,1)} %param.14) | copy-start | bytes 786436
  9.0 26.3 %copy-start.52 = (pred[128]{0:T(512)(128)(4,1)}, pred[128]{0:T(512)(128)(4,1)S(1)}, u32[]{:S(2)}) copy-start(pred[128]{0:T(512)(128)(4,1)S(1)} %get-tuple-element.77) | copy-start | bytes 388
  9.0 26.3 %copy-start.54 = (pred[128]{0:T(512)(128)(4,1)}, pred[128]{0:T(512)(128)(4,1)S(1)}, u32[]{:S(2)}) copy-start(pred[128]{0:T(512)(128)(4,1)S(1)} %get-tuple-element.75) | copy-start | bytes 388
  9.0 26.3 %copy-start.56 = (pred[128]{0:T(512)(128)(4,1)}, pred[128]{0:T(512)(128)(4,1)S(1)}, u32[]{:S(2)}) copy-start(pred[128]{0:T(512)(128)(4,1)S(1)} %get-tuple-element.63) | copy-start | bytes 388
  9.1 21.6 %copy-start.12 = (bf16[512,512]{1,0:T(8,128)(2,1)S(1)}, bf16[512,512]{1,0:T(8,128)(2,1)}, u32[]{:S(2)}) copy-start(bf16[512,512]{1,0:T(8,128)(2,1)} %param.19) | copy-start | bytes 1572868
  12.4 17.4 %all-to-all-start = ((bf16[8,32,512]{2,0,1:T(8,128)(2,1)}), bf16[8,32,512]{2,0,1:T(8,128)(2,1)S(1)}, u32[]{:S(2)}, u32[]{:S(2)}) async-start(bf16[8,32,512]{2,0,1:T(8,128)(2,1)} %copy.58), calls=%async_computation | async-start | bytes 524288 | tf_op jit(solution)/shard_map/all_to_all | solution.py:60
  19.8 199.0 %all-reduce.4.cloned.1.call-start = ((), (), s32[]{:S(2)}) async-start(), calls=%async_computation.2 | async-start | bytes 6651904 | tf_op jit(solution)/shard_map/psum | solution.py:159
  35.3 5.7 %copy-start.15 = (bf16[128,8,512]{2,1,0:T(8,128)(2,1)}, bf16[128,8,512]{2,1,0:T(8,128)(2,1)S(1)}, u32[]{:S(2)}) copy-start(bf16[128,8,512]{2,1,0:T(8,128)(2,1)S(1)} %gather_fusion.1) | copy-start | bytes 3145732
  47.0 4.1 %copy-start.51 = (s32[128]{0:T(128)S(1)}, s32[128]{0:T(128)}, u32[]{:S(2)}) copy-start(s32[128]{0:T(128)} %param.17) | copy-start | bytes 1540
  84.6 4.3 %copy-start.2 = (f32[8,128,512]{2,1,0:T(8,128)S(1)}, f32[8,128,512]{2,1,0:T(8,128)}, u32[]{:S(2)}) copy-start(f32[8,128,512]{2,1,0:T(8,128)} %copy-done.1) | copy-start | bytes 6291460
  84.6 4.3 %copy-start.35 = (bf16[512,83]{0,1:T(8,128)(2,1)S(1)}, bf16[512,83]{0,1:T(8,128)(2,1)}, u32[]{:S(2)}) copy-start(bf16[512,83]{0,1:T(8,128)(2,1)} %param.23) | copy-start | bytes 254980
  84.6 4.3 %copy-start.37 = (f32[8,128]{1,0:T(8,128)S(1)}, f32[8,128]{1,0:T(8,128)}, u32[]{:S(2)}) copy-start(f32[8,128]{1,0:T(8,128)} %copy-done.36) | copy-start | bytes 12292
  84.6 4.3 %copy-start.39 = (f32[8,128]{1,0:T(8,128)S(1)}, f32[8,128]{1,0:T(8,128)}, u32[]{:S(2)}) copy-start(f32[8,128]{1,0:T(8,128)} %copy-done.38) | copy-start | bytes 12292
  84.6 4.3 %copy-start.41 = (f32[8,128]{1,0:T(8,128)S(1)}, f32[8,128]{1,0:T(8,128)}, u32[]{:S(2)}) copy-start(f32[8,128]{1,0:T(8,128)} %copy-done.40) | copy-start | bytes 12292
  84.6 4.3 %copy-start.43 = (f32[8,128]{1,0:T(8,128)S(1)}, f32[8,128]{1,0:T(8,128)}, u32[]{:S(2)}) copy-start(f32[8,128]{1,0:T(8,128)} %copy-done.42) | copy-start | bytes 12292
  84.6 4.3 %copy-start.45 = (f32[8,128]{1,0:T(8,128)S(1)}, f32[8,128]{1,0:T(8,128)}, u32[]{:S(2)}) copy-start(f32[8,128]{1,0:T(8,128)} %copy-done.44) | copy-start | bytes 12292
  84.6 4.3 %copy-start.47 = (f32[512]{0:T(512)S(1)}, f32[512]{0:T(512)}, u32[]{:S(2)}) copy-start(f32[512]{0:T(512)} %param.22) | copy-start | bytes 6148
  88.9 4.5 %copy-start.4 = (f32[8,128,512]{2,1,0:T(8,128)S(1)}, f32[8,128,512]{2,1,0:T(8,128)}, u32[]{:S(2)}) copy-start(f32[8,128,512]{2,1,0:T(8,128)} %copy-done.3) | copy-start | bytes 6291460
  99.0 6.9 %copy-start.25 = (bf16[8,128,512]{2,1,0:T(8,128)(2,1)}, bf16[8,128,512]{2,1,0:T(8,128)(2,1)S(1)}, u32[]{:S(2)}) copy-start(bf16[8,128,512]{2,1,0:T(8,128)(2,1)S(1)} %multiply_convert_fusion) | copy-start | bytes 3145732
  100.7 5.1 %copy-start.26 = (bf16[8,128,512]{2,1,0:T(8,128)(2,1)}, bf16[8,128,512]{2,1,0:T(8,128)(2,1)S(1)}, u32[]{:S(2)}) copy-start(bf16[8,128,512]{2,1,0:T(8,128)(2,1)S(1)} %multiply_convert_fusion.2) | copy-start | bytes 3145732
  110.2 46.3 %copy-start.8 = (f32[8,128,512]{2,1,0:T(8,128)S(1)}, f32[8,128,512]{2,1,0:T(8,128)}, u32[]{:S(2)}) copy-start(f32[8,128,512]{2,1,0:T(8,128)} %copy-done.7) | copy-start | bytes 6291460
  113.8 46.4 %all-to-all-start.1 = ((bf16[8,32,512]{2,0,1:T(8,128)(2,1)}), bf16[8,32,512]{2,0,1:T(8,128)(2,1)S(1)}, u32[]{:S(2)}, u32[]{:S(2)}) async-start(bf16[8,32,512]{2,0,1:T(8,128)(2,1)} %copy.67), calls=%async_computation.1 | async-start | bytes 524288 | tf_op jit(solution)/shard_map/all_to_all | solution.py:151
  156.5 3.7 %copy-start.49 = (s32[32]{0:T(128)S(1)}, s32[32]{0:T(128)}, u32[]{:S(2)}) copy-start(s32[32]{0:T(128)} %copy-done.48) | copy-start | bytes 388
  (38 other events, 63.3 us)
Sparse Core Ops, SparseCore 0:
  110.3 108.3 all-reduce.3
where the time goes:
time: 233 us; the launch traced here: 232 us
  blocking collectives  69.4 us (30%)
  waiting for transfers between devices  66.5 us (29%)
  matrix products  35.1 us (15%)
  local copies, waits for them, and re-layouts  20.8 us (9%)
  between operations  18.1 us (8%)
  other arithmetic  11.2 us (5%)
  starting transfers between devices  10.9 us (5%)
    psum x2, blocking collectives, body(): lax.psum((jnp.sum(lat_weight), jnp.sum(lat_weight * jnp.sum(crps_value, a...  69.4 us
    psum x1, waiting for transfers between devices, body(): lax.psum((grad_send, grad_recv, grad_edge, grad_gain, head_matrix_sensiti...  56.5 us
    unnamed x124, local copies, waits for them, and re-layouts  12.2 us
    all_to_all x1, waiting for transfers between devices, body(): lax.all_to_all(jnp.take(mesh_latent, outgoing, axis=1), 'space', split_ax...  9.95 us
    all_to_all x1, starting transfers between devices, body(): lax.all_to_all(jnp.take(mesh_latent, outgoing, axis=1), 'space', split_ax...  7.36 us
    dot_general x1, matrix products, body(): jnp.einsum('mgl,lh->mgh', grid_latent, w_recv, preferred_element_type=jnp...  5.65 us
    dot_general x3, matrix products, body(): jnp.einsum('mgl,hl->mgh', dedge, w_edge, preferred_element_type=jnp.float32)  5.05 us
  transfers between devices with their start and end apart: 3, of which 2 were waited for; matrix products, arithmetic and copies ran while one was open for 4% of the time, Pallas kernels for 0%

commit v1 on v0

--- a/solution.py
+++ b/solution.py
@@ -1,6 +1,10 @@
+import functools
+
 import jax
 import jax.numpy as jnp
 from jax import lax
+from jax.experimental import pallas as pl
+from jax.experimental.pallas import tpu as pltpu
 from jax.sharding import PartitionSpec as P
 
 LATS = 721
@@ -37,6 +41,210 @@
     return jnp.einsum(
         "rs,msx->mrx", onehot, returned, preferred_element_type=jnp.float32, precision=PRECISE
     )
+
+
+MESH_ID = pl.DeviceIdType.MESH
+VMEM_LIMIT = 50 * 1024 * 1024
+
+
+def greet_all(me, n):
+    barrier = pltpu.get_barrier_semaphore()
+
+    @pl.loop(1, n)
+    def _(j):
+        pl.semaphore_signal(
+            barrier, inc=1, device_id={"space": lax.rem(me + j, n)}, device_id_type=MESH_ID
+        )
+
+    pl.semaphore_wait(barrier, n - 1)
+
+
+def swap_blocks(me, n, source, target, send_sem, recv_sem, blockwise):
+    @pl.loop(1, n)
+    def _(j):
+        peer = lax.rem(me + j, n)
+        pltpu.make_async_remote_copy(
+            src_ref=source.at[peer] if blockwise else source,
+            dst_ref=target.at[me],
+            send_sem=send_sem,
+            recv_sem=recv_sem,
+            device_id={"space": peer},
+            device_id_type=MESH_ID,
+        ).start()
+
+    span = target.at[pl.ds(0, n - 1)]
+    return pltpu.make_async_remote_copy(
+        src_ref=span,
+        dst_ref=span,
+        send_sem=send_sem,
+        recv_sem=recv_sem,
+        device_id={"space": lax.rem(me + 1, n)},
+        device_id_type=MESH_ID,
+    )
+
+
+def rows_kernel(n, sel_ref, mesh_ref, weight_ref, out_ref, weights_ref, outgoing, sems):
+    me = lax.axis_index("space")
+    greet_all(me, n)
+    swap_weights = swap_blocks(me, n, weight_ref, weights_ref, sems.at[0], sems.at[1], False)
+    weights_ref[me] = weight_ref[...]
+    slots, width = outgoing.shape[1], outgoing.shape[2]
+    sel = sel_ref[...]
+    pick = (sel == lax.broadcasted_iota(jnp.int32, (sel.shape[0], mesh_ref.shape[0]), 1)).astype(
+        jnp.bfloat16
+    )
+    rows = jnp.dot(pick, mesh_ref[...], preferred_element_type=jnp.float32).astype(jnp.bfloat16)
+    outgoing[...] = rows.reshape(n, slots, width)
+    swap_rows = swap_blocks(me, n, outgoing, out_ref, sems.at[2], sems.at[3], True)
+    out_ref[me] = outgoing[me]
+    swap_weights.wait()
+    swap_rows.wait()
+
+
+def exchange_rows(mesh_latent, send_rows, weight_part, n):
+    members, own_rows, width = mesh_latent.shape
+    cap = send_rows.shape[-1]
+    rows = send_rows.reshape(n, 1, cap) + own_rows * jnp.arange(members, dtype=jnp.int32)[None, :, None]
+    slots = members * cap
+    return pl.pallas_call(
+        functools.partial(rows_kernel, n),
+        out_shape=(
+            jax.ShapeDtypeStruct((n, slots, width), jnp.bfloat16),
+            jax.ShapeDtypeStruct((n, 8, 128), jnp.float32),
+        ),
+        in_specs=[pl.BlockSpec(memory_space=pltpu.VMEM)] * 3,
+        out_specs=[pl.BlockSpec(memory_space=pltpu.VMEM)] * 2,
+        scratch_shapes=[
+            pltpu.VMEM((n, slots, width), jnp.bfloat16),
+            pltpu.SemaphoreType.DMA((4,)),
+        ],
+        compiler_params=pltpu.CompilerParams(
+            collective_id=0, has_side_effects=True, vmem_limit_bytes=VMEM_LIMIT
+        ),
+    )(rows.reshape(n * slots, 1), mesh_latent.reshape(members * own_rows, width), weight_part)
+
+
+def stream_bits(n):
+    bits = [1 << k for k in range(n.bit_length() - 1)]
+    return [bits, bits[:1] + bits[2:] + bits[1:2]]
+
+
+def sum_kernel(
+    n, x_ref, slot_ref, loss_ref, out_ref, ret_ref, losses_ref, work, landed, send_sems, recv_sems, sems
+):
+    me = lax.axis_index("space")
+    greet_all(me, n)
+    streams = stream_bits(n)
+    steps = len(streams[0])
+    total = x_ref.shape[1]
+    low = [0] * len(streams)
+
+    def remote(src, dst, s, k, bit):
+        return pltpu.make_async_remote_copy(
+            src_ref=src,
+            dst_ref=dst,
+            send_sem=send_sems.at[s, k],
+            recv_sem=recv_sems.at[s, k],
+            device_id={"space": jnp.bitwise_xor(me, bit)},
+            device_id_type=MESH_ID,
+        )
+
+    def rows_at(start, size):
+        return pl.ds(pl.multiple_of(start, 16), size)
+
+    def halve(s, k):
+        bit = streams[s][k]
+        size = total >> (k + 1)
+        mine = lax.rem(me // bit, 2)
+        keep = low[s] + mine * size
+        give = low[s] + (1 - mine) * size
+        low[s] = keep
+        source = x_ref if k == 0 else work
+        copy = remote(
+            source.at[s, rows_at(give, size)],
+            landed.at[s, pl.ds(total - (total >> k), size)],
+            s,
+            k,
+            bit,
+        )
+        copy.start()
+        return copy
+
+    def add(s, k):
+        size = total >> (k + 1)
+        source = x_ref if k == 0 else work
+        target = out_ref if k == steps - 1 else work
+        kept = rows_at(low[s], size)
+        value = source[s, kept, :].astype(jnp.float32) + landed[
+            s, pl.ds(total - (total >> k), size), :
+        ].astype(jnp.float32)
+        target[s, kept, :] = value.astype(jnp.bfloat16)
+
+    def spread(s, k):
+        bit = streams[s][k]
+        size = total >> (k + 1)
+        block = out_ref.at[s, rows_at(low[s], size)]
+        copy = remote(block, block, s, 2 * steps - 1 - k, bit)
+        copy.start()
+        low[s] = low[s] - lax.rem(me // bit, 2) * size
+        return copy
+
+    copies = [halve(s, 0) for s in range(len(streams))]
+    swap_slots = swap_blocks(me, n, slot_ref, ret_ref, sems.at[0], sems.at[1], True)
+    swap_losses = swap_blocks(me, n, loss_ref, losses_ref, sems.at[2], sems.at[3], False)
+    ret_ref[me] = slot_ref[me]
+    losses_ref[me] = loss_ref[...]
+    for k in range(steps):
+        for s in range(len(streams)):
+            copies[s].wait()
+            add(s, k)
+            copies[s] = halve(s, k + 1) if k < steps - 1 else spread(s, k)
+    for k in reversed(range(steps)):
+        for s in range(len(streams)):
+            copies[s].wait()
+            if k > 0:
+                copies[s] = spread(s, k - 1)
+    swap_slots.wait()
+    swap_losses.wait()
+
+
+def sum_over_space(x, slots, loss, n):
+    streams = len(stream_bits(n))
+    steps = n.bit_length() - 1
+    return pl.pallas_call(
+        functools.partial(sum_kernel, n),
+        out_shape=(
+            jax.ShapeDtypeStruct(x.shape, x.dtype),
+            jax.ShapeDtypeStruct(slots.shape, slots.dtype),
+            jax.ShapeDtypeStruct((n,) + loss.shape, loss.dtype),
+        ),
+        in_specs=[pl.BlockSpec(memory_space=pltpu.VMEM)] * 3,
+        out_specs=[pl.BlockSpec(memory_space=pltpu.VMEM)] * 3,
+        scratch_shapes=[
+            pltpu.VMEM(x.shape, x.dtype),
+            pltpu.VMEM(x.shape, x.dtype),
+            pltpu.SemaphoreType.DMA((streams, 2 * steps)),
+            pltpu.SemaphoreType.DMA((streams, 2 * steps)),
+            pltpu.SemaphoreType.DMA((4,)),
+        ],
+        compiler_params=pltpu.CompilerParams(
+            collective_id=1, has_side_effects=True, vmem_limit_bytes=VMEM_LIMIT
+        ),
+    )(x, slots, loss)
+
+
+def corner(value):
+    return jnp.broadcast_to(value.reshape(1, 1), (8, 128)).astype(jnp.float32)
+
+
+def split_columns(parts, n):
+    rows = sum(part.shape[0] for part in parts)
+    total = -(-rows // (16 * n)) * 16 * n
+    width = parts[0].shape[1]
+    parts = parts + [jnp.zeros((total - rows, width), jnp.float32)]
+    stacked = jnp.concatenate([part.astype(jnp.bfloat16) for part in parts], axis=0)
+    half = width // 2
+    return jnp.stack([stacked[:, :half], stacked[:, half:]])
 
 
 def body(
@@ -57,9 +265,15 @@
     own_rows = mesh_latent.shape[1]
     peer_count = lax.axis_size("space")
     outgoing = send_rows.reshape(-1)
-    arrived = lax.all_to_all(
-        jnp.take(mesh_latent, outgoing, axis=1), "space", split_axis=1, concat_axis=1, tiled=True
-    )
+    cap = send_rows.shape[-1]
+    lat_weight = jnp.cos(jnp.pi * ((lat_row.astype(jnp.float32) + 0.5) / LATS - 0.5))
+    arrived, weight_parts = exchange_rows(
+        mesh_latent, send_rows, corner(jnp.sum(lat_weight)), peer_count
+    )
+    weight_sum = jnp.sum(weight_parts[:, 0, 0])
+    arrived = jnp.transpose(
+        arrived.reshape(peer_count, member_outputs, cap, -1), (1, 0, 2, 3)
+    ).reshape(member_outputs, peer_count * cap, -1)
     gathered = jnp.concatenate([mesh_latent, arrived], axis=1)
     lookup = project(gathered, w_send)
     receiver = jnp.einsum("mgl,lh->mgh", grid_latent, w_recv, preferred_element_type=jnp.float32)
@@ -84,15 +298,12 @@
     prognosis_values = jnp.einsum(
         "ozw,wd->odz", refreshed_latent, head_matrix, preferred_element_type=jnp.float32
     )
-    lat_weight = jnp.cos(jnp.pi * ((lat_row.astype(jnp.float32) + 0.5) / LATS - 0.5))
     accuracy_term = jnp.mean(softened_absolute(prognosis_values - verifying_analyses[None]), axis=0)
     member_spread = jnp.sum(
         softened_absolute(prognosis_values[:, None] - prognosis_values[None, :]), axis=(0, 1)
     ) / (2.0 * member_outputs * (member_outputs - 1))
     crps_value = accuracy_term - member_spread
-    weight_sum, weighted = lax.psum(
-        (jnp.sum(lat_weight), jnp.sum(lat_weight * jnp.sum(crps_value, axis=0))), "space"
-    )
+    weighted = jnp.sum(lat_weight * jnp.sum(crps_value, axis=0))
     dispersion_factor = lat_weight * (points * peer_count / weight_sum)
     couple_derivative = jnp.sum(
         smooth_sign_function(prognosis_values[:, None] - prognosis_values[None, :]), axis=1
@@ -102,7 +313,7 @@
         * (smooth_sign_function(prognosis_values - verifying_analyses[None]) - couple_derivative)
     ).astype(jnp.bfloat16)
     head_matrix_sensitivity = jnp.einsum(
-        "wuj,wru->jr", refreshed_latent, prognosis_sensitivity, preferred_element_type=jnp.float32
+        "wru,wuj->rj", prognosis_sensitivity, refreshed_latent, preferred_element_type=jnp.float32
     )
     refreshed_latent_adjoint = jnp.einsum(
         "ord,ur->odu", prognosis_sensitivity, head_matrix, preferred_element_type=jnp.float32
@@ -148,18 +359,25 @@
     ).astype(jnp.bfloat16)
     grad_send = jnp.einsum("mtl,mth->lh", gathered, dslot, preferred_element_type=jnp.float32)
     grad_lat = jnp.einsum("mth,lh->mtl", dslot, w_send, preferred_element_type=jnp.float32)
-    returned = lax.all_to_all(
-        grad_lat[:, own_rows:].astype(jnp.bfloat16),
-        "space",
-        split_axis=1,
-        concat_axis=1,
-        tiled=True,
-    ).astype(jnp.float32)
-    grad_mesh = grad_lat[:, :own_rows] + fold_rows(returned, outgoing, own_rows)
-    totals = lax.psum(
-        (grad_send, grad_recv, grad_edge, grad_gain, head_matrix_sensitivity), "space"
-    )
-    loss_value = (weighted / weight_sum).reshape(1)
+    slots = jnp.transpose(
+        grad_lat[:, own_rows:].astype(jnp.bfloat16).reshape(member_outputs, peer_count, cap, -1),
+        (1, 0, 2, 3),
+    ).reshape(peer_count, member_outputs * cap, -1)
+    parts = [grad_send, grad_recv, grad_edge, grad_gain[None], head_matrix_sensitivity]
+    sums, returned, losses = sum_over_space(
+        split_columns(parts, peer_count), slots, corner(weighted), peer_count
+    )
+    returned = jnp.transpose(
+        returned.reshape(peer_count, member_outputs, cap, -1), (1, 0, 2, 3)
+    ).reshape(member_outputs, peer_count * cap, -1)
+    grad_mesh = grad_lat[:, :own_rows] + fold_rows(returned.astype(jnp.float32), outgoing, own_rows)
+    sums = jnp.concatenate([sums[0], sums[1]], axis=1).astype(jnp.float32)
+    totals = []
+    start = 0
+    for part in parts:
+        totals.append(sums[start : start + part.shape[0]])
+        start += part.shape[0]
+    loss_value = (jnp.sum(losses[:, 0, 0]) / weight_sum).reshape(1)
     return (
         loss_value,
         grad_grid,
@@ -167,8 +385,8 @@
         totals[0],
         totals[1],
         totals[2],
-        totals[3],
-        totals[4],
+        totals[3][0],
+        totals[4].T,
     )
 
 

time: 233 us -> 133 us (0.57)
  blocking collectives: 69.4 us -> 0 us
  waiting for transfers between devices: 66.5 us -> 0 us
  Pallas kernels: 0 us -> 58.8 us
  between operations: 18.1 us -> 4.62 us
  starting transfers between devices: 10.9 us -> 0 us
  other arithmetic: 11.2 us -> 17 us
  matrix products: 35.1 us -> 31.5 us
    psum x2 -> x0, blocking collectives: 69.4 us -> none  [body(): lax.psum((jnp.sum(lat_weight), jnp.sum(lat_weight * jnp.sum(crps_value, a...]
    pallas_call x0 -> x2, Pallas kernels: none -> 58.8 us  [the longest x1 46.5 us: sum_over_space(): pl.pallas_call(functools.partial(sum_kernel, n), out_shape=(jax.ShapeDtyp...]
    psum x1 -> x0, waiting for transfers between devices: 56.5 us -> none  [body(): lax.psum((grad_send, grad_recv, grad_edge, grad_gain, head_matrix_sensiti...]
    all_to_all x2 -> x0, starting transfers between devices: 10.9 us -> none  [the longest x1 7.36 us: body(): lax.all_to_all(jnp.take(mesh_latent, outgoing, axis=1), 'space', split_ax...]
    all_to_all x2 -> x0, waiting for transfers between devices: 9.95 us -> none  [the longest x1 9.95 us: body(): lax.all_to_all(jnp.take(mesh_latent, outgoing, axis=1), 'space', split_ax...]
    unnamed x124 -> x106, local copies, waits for them, and re-layouts: 12.2 us -> 6.26 us
    concatenate x0 -> x1, local copies, waits for them, and re-layouts: none -> 4.62 us  [split_columns(): jnp.concatenate([part.astype(jnp.bfloat16) for part in parts], axis=0)]
    reduce_sum x2 -> x6, other arithmetic: 2.96 us -> 5.88 us  [the longest x1 2.36 us: body(): jnp.sum(softened_absolute(prognosis_values[:, None] - prognosis_values[No...]
  transfers between devices with their start and end apart: 3 -> 0, of which waited for: 2 -> 0; matrix products, arithmetic and copies ran while one was open for 4% -> 0% of each run, Pallas kernels for 0% -> 0%
where the time goes in v1:
time: 133 us
  Pallas kernels  58.8 us (44%)
  matrix products  31.5 us (24%)
  local copies, waits for them, and re-layouts  20.6 us (15%)
  other arithmetic  17 us (13%)
  between operations  4.62 us (3%)
    pallas_call x1, Pallas kernels, sum_over_space(): pl.pallas_call(functools.partial(sum_kernel, n), out_shape=(jax.ShapeDtyp...  46.5 us
    pallas_call x1, Pallas kernels, exchange_rows(): pl.pallas_call(functools.partial(rows_kernel, n), out_shape=(jax.ShapeDty...  12.3 us
    unnamed x106, local copies, waits for them, and re-layouts  6.26 us
    dot_general x1, matrix products, body(): jnp.einsum('mgl,lh->mgh', grid_latent, w_recv, preferred_element_type=jnp...  5.33 us
    dot_general x3, matrix products, body(): jnp.einsum('mgl,hl->mgh', dedge, w_edge, preferred_element_type=jnp.float32)  5.06 us
    concatenate x1, local copies, waits for them, and re-layouts, split_columns(): jnp.concatenate([part.astype(jnp.bfloat16) for part in parts], axis=0)  4.62 us
    dot_general x1, matrix products, body(): jnp.einsum('ord,ur->odu', prognosis_sensitivity, head_matrix, preferred_e...  4.5 us
    gather x3, local copies, waits for them, and re-layouts, body(): jnp.take(lookup, edge_slot[edge_index], axis=1).astype(jnp.float32)  3.87 us

profile of v1, /device:TPU:0, one launch (start us, length us, event | category | flops | bytes accessed | tf_op | source)
XLA Modules:
  0.0 132.5 jit_solution(4585242207612143527)
XLA Ops:
  1.5 1.8 %fusion.52 = (f32[]{:T(128)}, f32[128]{0:T(128)}) fusion(s32[128]{0:T(128)} %param.17), kind=kLoop, calls=%fused_computation.138 | loop fusion | flops 767 | bytes 1028 | tf_op jit(solution)/shard_map/reduce_sum | solution.py:271
  4.9 0.9 copy-done.1
  5.9 12.3 %shard_map.170 = (bf16[16,16,512]{2,1,0:T(8,128)(2,1)S(1)}, f32[16,8,128]{2,1,0:T(8,128)S(1)}) custom-call(s32[256,1]{1,0:T(8,128)S(1)} %add.190.sel_ref, bf16[256,512]{1,0:T(8,128)(2,1)S(1)} %bitcast.143, f32[8,128]{1,0:T(8,128)S(1)} %broadcast_in_dim.15.weight_ref), custom_call_target="tpu_custom_call" | custom-call | tf_op jit(solution)/shard_map/pallas_call | solution.py:109
  20.1 1.6 %gather_fusion.1 = bf16[128,8,512]{2,1,0:T(8,128)(2,1)} fusion(bf16[8,64,512]{2,0,1:T(8,128)(2,1)S(1)} %copy.47, s32[1024]{0:T(1024)S(1)} %get-tuple-element.68), kind=kCustom, calls=%fused_computation.1.clone | custom fusion | bytes 2097664 | tf_op jit(solution)/shard_map/jit(_take)/gather | solution.py:286
  21.7 1.6 %gather_fusion = bf16[128,8,512]{2,1,0:T(8,128)(2,1)} fusion(bf16[8,64,512]{2,0,1:T(8,128)(2,1)S(1)} %copy.47, s32[1024]{0:T(1024)S(1)} %pad_clamp_fusion.2), kind=kCustom, calls=%fused_computation.clone | custom fusion | bytes 2097664 | tf_op jit(solution)/shard_map/jit(_take)/gather | solution.py:286
  23.4 5.3 %multiply_convert_fusion.7 = (bf16[8,128,512]{2,1,0:T(8,128)(2,1)S(1)}, bf16[8,128,512]{2,1,0:T(8,128)(2,1)S(1)}, bf16[8,128,512]{2,1,0:T(8,128)(2,1)S(1)}, f32[8,128,512]{2,1,0:T(8,128)}) fusion(bf16[128,8,512]{2,1,0:T(8,128)(2,1)} %gather_fusion.1, pred[128]{0:T(512)(128)(4,1)S(1)} %get-tuple-element.32, bf16[128,8,512]{2,1,0:T(8,128)(2,1)S(1)} %gather_fusion.2, ...), kind=kOutput, calls=%fused_computation.36 | convolution fusion | flops 549453824 | bytes 9961856 | tf_op jit(solution)/shard_map/mgl,lh->mgh/dot_general | solution.py:279
  33.4 1.1 fusion.10
  35.6 2.4 %fusion.8 = (f32[83,128]{1,0:T(8,128)}, f32[8,83,128]{2,1,0:T(8,128)S(1)}) fusion(f32[8,83,128]{2,0,1:T(8,128)S(1)} %copy.53, f32[8,83,128]{2,1,0:T(8,128)S(1)} %convolution_bitcast_fusion.6), kind=kLoop, calls=%fused_computation.13 | loop fusion | flops 3984000 | bytes 1062400 | tf_op jit(solution)/shard_map/reduce_sum | solution.py:302
  41.2 1.3 multiply_reduce_fusion.10
  43.1 1.5 %fusion.25 = bf16[83,512]{1,0:T(8,128)(2,1)S(1)} fusion(bf16[8,83,128]{2,1,0:T(8,128)(2,1)S(1)} %get-tuple-element.54, bf16[8,128,512]{2,1,0:T(8,128)(2,1)} %copy-done.7), kind=kOutput, calls=%fused_computation.68 | convolution fusion | flops 87074304 | bytes 1303552 | tf_op jit(solution)/shard_map/wru,wuj->rj/dot_general | solution.py:315
  44.7 4.5 %multiply_reduce_fusion = (f32[512]{0:T(512)S(1)}, f32[8,128]{1,0:T(8,128)S(1)}, f32[8,128]{1,0:T(8,128)S(1)}, f32[512]{0:T(512)S(1)}, f32[8,128]{1,0:T(8,128)S(...) fusion(f32[8,128,512]{2,1,0:T(8,128)} %copy-done.5, f32[8,128]{1,0:T(8,128)} %copy-done.39, ...), kind=kOutput, calls=%fused_computation.18 | convolution fusion | flops 97511936 | bytes 8692736 | tf_op jit(solution)/shard_map/ord,ur->odu/dot_general | solution.py:318
  49.3 2.0 %multiply_convert_fusion.5 = (bf16[8,128,512]{2,1,0:T(8,128)(2,1)S(1)}, bf16[8,128,512]{2,1,0:T(8,128)(2,1)S(1)}, bf16[8,128,512]{2,1,0:T(8,128)(2,1)S(1)}) fusion(f32[8,128,512]{2,1,0:T(8,128)S(1)} %get-tuple-element.65, f32[8,128,512]{2,1,0:T(8,128)S(1)} %get-tuple-element.66, f32[8,128]{1,0:T(8,128)S(1)} %broadcast_multiply_fusion.2, ...), kind=kLoop, calls=%fused_computation.29 | loop fusion | flops 10485760 | bytes 11577344 | tf_op jit(solution)/shard_map/convert_element_type | solution.py:334
  55.7 1.7 %multiply_convert_fusion.4 = bf16[8,128,512]{2,1,0:T(8,128)(2,1)S(1)} fusion(bf16[8,128,512]{2,1,0:T(8,128)(2,1)S(1)} %get-tuple-element.43, f32[8,128,512]{2,1,0:T(8,128)S(1)} %copy-done.51, bf16[512,512]{1,0:T(8,128)(2,1)S(1)} %copy-done, bf16[128,8,512]{2,1,0:T(8,128)(2,1)S(1)} %copy-done.20, pred[128]{0:T(512)(128)(4,1)S(1)} %copy-done.50), kind=kOutput, calls=%fused_computation.28 | convolution fusion | flops 543162368 | bytes 5767296 | tf_op jit(solution)/shard_map/mgl,hl->mgh/dot_general | solution.py:338
  57.5 1.7 %multiply_convert_fusion.2 = bf16[8,128,512]{2,1,0:T(8,128)(2,1)S(1)} fusion(bf16[8,128,512]{2,1,0:T(8,128)(2,1)S(1)} %get-tuple-element.45, f32[8,128,512]{2,1,0:T(8,128)S(1)} %copy-done.51, bf16[512,512]{1,0:T(8,128)(2,1)S(1)} %copy-done, bf16[128,8,512]{2,1,0:T(8,128)(2,1)S(1)} %copy-done.19, pred[128]{0:T(512)(128)(4,1)S(1)} %copy-done.48), kind=kOutput, calls=%fused_computation.25 | convolution fusion | flops 543162368 | bytes 5767296 | tf_op jit(solution)/shard_map/mgl,hl->mgh/dot_general | solution.py:338
  59.2 1.7 %multiply_convert_fusion = bf16[8,128,512]{2,1,0:T(8,128)(2,1)S(1)} fusion(bf16[8,128,512]{2,1,0:T(8,128)(2,1)S(1)} %get-tuple-element.44, f32[8,128,512]{2,1,0:T(8,128)S(1)} %copy-done.51, bf16[512,512]{1,0:T(8,128)(2,1)S(1)} %copy-done, bf16[128,8,512]{2,1,0:T(8,128)(2,1)S(1)} %copy-done.18, pred[128]{0:T(512)(128)(4,1)S(1)} %copy-done.46), kind=kOutput, calls=%fused_computation.22 | convolution fusion | flops 543162368 | bytes 5767296 | tf_op jit(solution)/shard_map/mgl,hl->mgh/dot_general | solution.py:338
  60.9 1.6 %fusion.19 = bf16[512,512]{1,0:T(8,128)(2,1)} fusion(bf16[8,128,512]{2,1,0:T(8,128)(2,1)S(1)} %copy-done.29, bf16[8,128,512]{2,1,0:T(8,128)(2,1)S(1)} %multiply_convert_fusion, bf16[8,128,512]{2,1,0:T(8,128)(2,1)S(1)} %multiply_convert_fusion.2, bf16[8,128,512]{2,1,0:T(8,128)(2,1)S(1)} %multiply_convert_fusion.4), kind=kOutput, calls=%fused_computation.61 | convolution fusion | flops 540278784 | bytes 4718592 | tf_op jit(solution)/shard_map/mgl,mgh->lh/dot_general | solution.py:347
  63.6 1.3 fusion.18
  64.9 4.6 %concatenate.14 = bf16[1792,512]{1,0:T(8,128)(2,1)S(1)} concatenate(bf16[512,512]{1,0:T(8,128)(2,1)} %fusion.18, bf16[512,512]{1,0:T(8,128)(2,1)} %fusion.19, bf16[512,512]{1,0:T(8,128)(2,1)S(1)} %fusion.17, bf16[1,512]{1,0:T(2,128)(2,1)S(1)} %convert_element_type.141, bf16[83,512]{1,0:T(8,128)(2,1)S(1)} %fusion.25, bf16[172,512]{1,0:T(8,128)(2,1)S(1)} %broadcast_in_dim.16), dimensions={0} | concatenate | bytes 3670016 | tf_op jit(solution)/shard_map/concatenate | solution.py:245
  69.7 1.4 %pad_maximum_fusion.x_ref = bf16[2,1792,256]{2,1,0:T(8,128)(2,1)} fusion(bf16[1,1792,256]{2,1,0:T(8,128)(2,1)S(1)} %get-tuple-element.52, bf16[1,1792,256]{2,1,0:T(8,128)(2,1)S(1)} %get-tuple-element.51), kind=kLoop, calls=%fused_computation.46 | loop fusion | flops 917504 | bytes 3670016 | tf_op jit(solution)/shard_map/stack | solution.py:247
  71.6 1.0 copy-done.12
  73.1 46.5 %shard_map.171 = (bf16[2,1792,256]{2,1,0:T(8,128)(2,1)S(1)}, bf16[16,16,512]{2,1,0:T(8,128)(2,1)S(1)}, f32[16,8,128]{2,1,0:T(8,128)S(1)}) custom-call(bf16[2,1792,256]{2,1,0:T(8,128)(2,1)} %pad_maximum_fusion.x_ref, bf16[16,16,512]{2,1,0:T(8,128)(2,1)S(1)} %reshape.167.slot_ref, f32[8,128]{1,0:T(8,128)S(1)} %broadcast_in_dim.17.loss_ref), custom_call_target="tpu_custom_call" | custom-call | tf_op jit(solution)/shard_map/pallas_call | solution.py:214
  121.5 1.7 %fusion.53 = (f32[512,512]{1,0:T(8,128)}, f32[512,512]{1,0:T(8,128)}, f32[512,512]{1,0:T(8,128)}) fusion(f32[1792,512]{1,0:T(8,128)S(1)} %maximum_convert_fusion), kind=kLoop, calls=%fused_computation.139 | loop fusion | bytes 6291456 | tf_op jit(solution)/shard_map/slice | solution.py:378
  123.8 2.0 %fusion.24 = bf16[8,32,512]{2,1,0:T(8,128)(2,1)} fusion(bf16[8,32,512]{2,1,0:T(8,128)(2,1)S(1)} %reshape.170, f32[8,64,512]{2,1,0:T(8,128)} %copy-done.12, s32[32]{0:T(128)S(1)} %eq.34), kind=kOutput, calls=%fused_computation.65 | convolution fusion | flops 8651776 | bytes 1048704 | tf_op jit(solution)/shard_map/rs,msx->mrx/dot_general | solution.py:41
  125.8 3.7 %add_convert_fusion = bf16[8,128,512]{2,1,0:T(8,128)(2,1)} fusion(f32[8,128,512]{2,1,0:T(8,128)S(1)} %copy-done.9, bf16[512,512]{1,0:T(8,128)(2,1)} %param.20, bf16[8,128,512]{2,1,0:T(8,128)(2,1)} %copy-done.27, bf16[8,128,512]{2,1,0:T(8,128)(2,1)} %copy-done.26, bf16[8,128,512]{2,1,0:T(8,128)(2,1)} %copy-done.25), kind=kOutput, calls=%fused_computation.17 | convolution fusion | flops 541065216 | bytes 6815744 | tf_op jit(solution)/shard_map/mgh,lh->mgl/dot_general | solution.py:345
  (164 shorter events, 22.7 us)
Async XLA Ops:
  0.6 28.1 %copy-start = (bf16[512,512]{1,0:T(8,128)(2,1)S(1)}, bf16[512,512]{1,0:T(8,128)(2,1)}, u32[]{:S(2)}) copy-start(bf16[512,512]{1,0:T(8,128)(2,1)} %param.21) | copy-start | bytes 1572868
  0.6 18.0 %copy-start.2 = (bf16[8,32,512]{2,1,0:T(8,128)(2,1)S(1)}, bf16[8,32,512]{2,1,0:T(8,128)(2,1)}, u32[]{:S(2)}) copy-start(bf16[8,32,512]{2,1,0:T(8,128)(2,1)} %param.14) | copy-start | bytes 786436
  1.5 21.9 %copy-start.45 = (pred[128]{0:T(512)(128)(4,1)}, pred[128]{0:T(512)(128)(4,1)S(1)}, u32[]{:S(2)}) copy-start(pred[128]{0:T(512)(128)(4,1)S(1)} %get-tuple-element.57) | copy-start | bytes 388
  1.5 21.9 %copy-start.47 = (pred[128]{0:T(512)(128)(4,1)}, pred[128]{0:T(512)(128)(4,1)S(1)}, u32[]{:S(2)}) copy-start(pred[128]{0:T(512)(128)(4,1)S(1)} %get-tuple-element.32) | copy-start | bytes 388
  1.5 21.9 %copy-start.49 = (pred[128]{0:T(512)(128)(4,1)}, pred[128]{0:T(512)(128)(4,1)S(1)}, u32[]{:S(2)}) copy-start(pred[128]{0:T(512)(128)(4,1)S(1)} %get-tuple-element.55) | copy-start | bytes 388
  5.9 12.8 %copy-start.13 = (bf16[512,512]{1,0:T(8,128)(2,1)S(1)}, bf16[512,512]{1,0:T(8,128)(2,1)}, u32[]{:S(2)}) copy-start(bf16[512,512]{1,0:T(8,128)(2,1)} %param.19) | copy-start | bytes 1572868
  20.1 3.3 %copy-start.17 = (bf16[128,8,512]{2,1,0:T(8,128)(2,1)}, bf16[128,8,512]{2,1,0:T(8,128)(2,1)S(1)}, u32[]{:S(2)}) copy-start(bf16[128,8,512]{2,1,0:T(8,128)(2,1)S(1)} %gather_fusion.2) | copy-start | bytes 3145732
  20.1 3.3 %copy-start.32 = (bf16[512,512]{1,0:T(8,128)(2,1)S(1)}, bf16[512,512]{1,0:T(8,128)(2,1)}, u32[]{:S(2)}) copy-start(bf16[512,512]{1,0:T(8,128)(2,1)} %param.20) | copy-start | bytes 1572868
  28.7 2.6 %copy-start.21 = (bf16[8,128,512]{2,1,0:T(8,128)(2,1)}, bf16[8,128,512]{2,1,0:T(8,128)(2,1)S(1)}, u32[]{:S(2)}) copy-start(bf16[8,128,512]{2,1,0:T(8,128)(2,1)S(1)} %get-tuple-element.47) | copy-start | bytes 3145732
  30.0 2.6 %copy-start.35 = (f32[8,128]{1,0:T(8,128)}, f32[8,128]{1,0:T(8,128)S(1)}, u32[]{:S(2)}) copy-start(f32[8,128]{1,0:T(8,128)S(1)} %add_rsqrt_fusion.2) | copy-start | bytes 12292
  31.3 2.1 %copy-start.28 = (bf16[8,128,512]{2,1,0:T(8,128)(2,1)S(1)}, bf16[8,128,512]{2,1,0:T(8,128)(2,1)}, u32[]{:S(2)}) copy-start(bf16[8,128,512]{2,1,0:T(8,128)(2,1)} %param.13) | copy-start | bytes 3145732
  32.1 2.4 %copy-start.5 = (f32[8,128,512]{2,1,0:T(8,128)}, f32[8,128,512]{2,1,0:T(8,128)S(1)}, u32[]{:S(2)}) copy-start(f32[8,128,512]{2,1,0:T(8,128)S(1)} %get-tuple-element.61) | copy-start | bytes 6291460
  34.5 5.6 %copy-start.34 = (f32[83,128]{1,0:T(8,128)S(1)}, f32[83,128]{1,0:T(8,128)}, u32[]{:S(2)}) copy-start(f32[83,128]{1,0:T(8,128)} %param.18) | copy-start | bytes 127492
  39.3 5.3 %copy-start.4 = (f32[8,128,512]{2,1,0:T(8,128)S(1)}, f32[8,128,512]{2,1,0:T(8,128)}, u32[]{:S(2)}) copy-start(f32[8,128,512]{2,1,0:T(8,128)} %copy-done.3) | copy-start | bytes 6291460
  44.6 4.6 %copy-start.6 = (f32[8,128,512]{2,1,0:T(8,128)S(1)}, f32[8,128,512]{2,1,0:T(8,128)}, u32[]{:S(2)}) copy-start(f32[8,128,512]{2,1,0:T(8,128)} %copy-done.5) | copy-start | bytes 6291460
  44.6 4.6 %copy-start.36 = (f32[8,128]{1,0:T(8,128)S(1)}, f32[8,128]{1,0:T(8,128)}, u32[]{:S(2)}) copy-start(f32[8,128]{1,0:T(8,128)} %copy-done.35) | copy-start | bytes 12292
  44.6 4.6 %copy-start.38 = (f32[8,128]{1,0:T(8,128)S(1)}, f32[8,128]{1,0:T(8,128)}, u32[]{:S(2)}) copy-start(f32[8,128]{1,0:T(8,128)} %copy-done.37) | copy-start | bytes 12292
  44.6 4.6 %copy-start.40 = (f32[8,128]{1,0:T(8,128)S(1)}, f32[8,128]{1,0:T(8,128)}, u32[]{:S(2)}) copy-start(f32[8,128]{1,0:T(8,128)} %copy-done.39) | copy-start | bytes 12292
  44.7 4.6 %copy-start.42 = (f32[512]{0:T(512)S(1)}, f32[512]{0:T(512)}, u32[]{:S(2)}) copy-start(f32[512]{0:T(512)} %param.22) | copy-start | bytes 6148
  49.2 2.1 %copy-start.8 = (f32[8,128,512]{2,1,0:T(8,128)}, f32[8,128,512]{2,1,0:T(8,128)S(1)}, u32[]{:S(2)}) copy-start(f32[8,128,512]{2,1,0:T(8,128)S(1)} %get-tuple-element.66) | copy-start | bytes 6291460
  57.4 5.1 %copy-start.25 = (bf16[8,128,512]{2,1,0:T(8,128)(2,1)}, bf16[8,128,512]{2,1,0:T(8,128)(2,1)S(1)}, u32[]{:S(2)}) copy-start(bf16[8,128,512]{2,1,0:T(8,128)(2,1)S(1)} %multiply_convert_fusion.4) | copy-start | bytes 3145732
  59.2 3.4 %copy-start.26 = (bf16[8,128,512]{2,1,0:T(8,128)(2,1)}, bf16[8,128,512]{2,1,0:T(8,128)(2,1)S(1)}, u32[]{:S(2)}) copy-start(bf16[8,128,512]{2,1,0:T(8,128)(2,1)S(1)} %multiply_convert_fusion.2) | copy-start | bytes 3145732
  121.5 2.2 %copy-start.43 = (s32[1,16,2]{1,2,0:T(2,128)S(1)}, s32[1,16,2]{1,2,0:T(2,128)}, u32[]{:S(2)}) copy-start(s32[1,16,2]{1,2,0:T(2,128)} %param.15) | copy-start | bytes 388
  123.2 2.6 %copy-start.9 = (f32[8,128,512]{2,1,0:T(8,128)S(1)}, f32[8,128,512]{2,1,0:T(8,128)}, u32[]{:S(2)}) copy-start(f32[8,128,512]{2,1,0:T(8,128)} %copy-done.8) | copy-start | bytes 6291460
  (28 other events, 39.9 us)

commit v2 on v1

--- a/solution.py
+++ b/solution.py
@@ -13,25 +13,6 @@
 DELTA_SQ = 0.0025
 NORM_EPS = 1e-05
 PRECISE = lax.Precision.HIGHEST
-
-
-def softened_absolute(offset):
-    return jnp.sqrt(offset * offset + DELTA_SQ)
-
-
-def smooth_sign_function(offset):
-    return offset / jnp.sqrt(offset * offset + DELTA_SQ)
-
-
-def silu_slope(offset):
-    logistic = jax.nn.sigmoid(offset)
-    return logistic * (1.0 + offset * (1.0 - logistic))
-
-
-def project(node_rows, weight):
-    return jnp.einsum("mrl,lh->mrh", node_rows, weight, preferred_element_type=jnp.float32).astype(
-        jnp.bfloat16
-    )
 
 
 def fold_rows(returned, row_ids, row_count):
@@ -233,18 +214,262 @@
     )(x, slots, loss)
 
 
+TN = (((0,), (0,)), ((), ()))
+NT = (((1,), (1,)), ((), ()))
+
+
+def mxu(left, right, dims=(((1,), (0,)), ((), ()))):
+    return lax.dot_general(left, right, dims, preferred_element_type=jnp.float32)
+
+
+def local_kernel(
+    channels,
+    grid_total,
+    grid_ref,
+    table_ref,
+    slot_ref,
+    lat_ref,
+    weights_ref,
+    target_ref,
+    w_send_ref,
+    w_recv_ref,
+    w_edge_ref,
+    gain_ref,
+    head_ref,
+    grad_grid_ref,
+    own_ref,
+    away_ref,
+    sums_ref,
+    loss_ref,
+    sender,
+    slope,
+    normed,
+    inv_std,
+    hidden,
+    updated,
+    forecast,
+    dforecast,
+    dedge,
+    dreceiver,
+    dslot,
+    pick,
+    edge_total,
+):
+    members, points, width = grid_ref.shape
+    slots = table_ref.shape[1]
+    own_rows = own_ref.shape[1]
+    edges = slot_ref.shape[0]
+    gain = gain_ref[...]
+    half = width // 2
+
+    for e in range(edges):
+        row = slot_ref[pl.ds(e, 1), :]
+        pick[:, e * points : (e + 1) * points] = (
+            lax.broadcasted_iota(jnp.int32, (slots, points), 0) == row
+        ).astype(jnp.bfloat16)
+
+    group = max(1, min(members, 512 // slots))
+    while members % group:
+        group -= 1
+
+    @pl.loop(0, members // group)
+    def _(t):
+        rows = table_ref[pl.ds(t * group, group)].reshape(group * slots, width)
+        sent = mxu(rows, w_send_ref[...]).astype(jnp.bfloat16)
+        sender[pl.ds(t * group, group)] = sent.reshape(group, slots, width)
+
+    @pl.loop(0, members)
+    def _(m):
+        latent = grid_ref[m]
+        receiver = mxu(latent, w_recv_ref[...])
+        v = mxu(pick[...], sender[m], TN) + jnp.concatenate([receiver] * edges, axis=0)
+        s = 0.5 * jnp.tanh(0.5 * v) + 0.5
+        act = v * s
+        slope[m] = s + act * (1.0 - s)
+        act = act.astype(jnp.bfloat16)
+        hidden[m] = act
+        out = mxu(act, w_edge_ref[...])
+        centred = out - jnp.mean(out, axis=-1, keepdims=True)
+        inv = lax.rsqrt(jnp.mean(centred * centred, axis=-1, keepdims=True) + NORM_EPS)
+        scaled = centred * inv
+        normed[m] = scaled
+        inv_std[m] = inv
+        summed = scaled[:points]
+        for e in range(1, edges):
+            summed = summed + scaled[e * points : (e + 1) * points]
+        fresh = (latent.astype(jnp.float32) + summed * gain).astype(jnp.bfloat16)
+        updated[m] = fresh
+        forecast[m] = mxu(fresh, head_ref[...])
+
+    weight_sum = jnp.sum(weights_ref[...], axis=0)[:1, :]
+    factor_scale = grid_total / weight_sum
+    chunk = 16
+    lanes = forecast.shape[2]
+    real = lax.broadcasted_iota(jnp.int32, (chunk, lanes), 1) < channels
+
+    def score(t, total):
+        rows = pl.ds(pl.multiple_of(t * chunk, chunk), chunk)
+        weight = lat_ref[rows, :]
+        target = target_ref[rows, :]
+        values = [forecast[m, rows, :] for m in range(members)]
+        accuracy = jnp.zeros((chunk, lanes), jnp.float32)
+        spread = jnp.zeros((chunk, lanes), jnp.float32)
+        signs = []
+        for m in range(members):
+            offset = values[m] - target
+            square = offset * offset + DELTA_SQ
+            root = lax.rsqrt(square)
+            accuracy = accuracy + square * root
+            signs.append(offset * root)
+        couples = [jnp.zeros((chunk, lanes), jnp.float32) for _ in range(members)]
+        for m in range(members):
+            for k in range(m + 1, members):
+                offset = values[m] - values[k]
+                square = offset * offset + DELTA_SQ
+                root = lax.rsqrt(square)
+                spread = spread + square * root
+                sign = offset * root
+                couples[m] = couples[m] + sign
+                couples[k] = couples[k] - sign
+        spread = (2.0 * spread + members * DELTA_SQ**0.5) / (2.0 * members * (members - 1))
+        crps = jnp.where(real, weight * (accuracy / members - spread), 0.0)
+        factor = weight * factor_scale
+        for m in range(members):
+            dforecast[m, rows, :] = (factor * (signs[m] - couples[m] / (members - 1))).astype(
+                jnp.bfloat16
+            )
+        return total + crps
+
+    total = lax.fori_loop(0, points // chunk, score, jnp.zeros((chunk, lanes), jnp.float32))
+    total = jnp.sum(jnp.sum(total, axis=1, keepdims=True), axis=0, keepdims=True)
+    loss_ref[...] = jnp.broadcast_to(total, loss_ref.shape)
+
+    def backward(m, gain_total):
+        dupdated = mxu(dforecast[m], head_ref[...], NT)
+        scaled_grad = dupdated * gain
+        shifted = scaled_grad - jnp.mean(scaled_grad, axis=-1, keepdims=True)
+        norm_sum = jnp.zeros((points, width), jnp.float32)
+        for e in range(edges):
+            rows = slice(e * points, (e + 1) * points)
+            norm = normed[m, rows, :]
+            norm_sum = norm_sum + norm
+            slant = jnp.mean(scaled_grad * norm, axis=-1, keepdims=True)
+            dedge[m, rows, :] = (inv_std[m, rows, :] * (shifted - norm * slant)).astype(jnp.bfloat16)
+        gain_total = gain_total + jnp.sum(dupdated * norm_sum, axis=0, keepdims=True)
+        dhidden = mxu(dedge[m], w_edge_ref[...], NT)
+        dpre = (dhidden * slope[m]).astype(jnp.bfloat16)
+        drecv = dpre[:points].astype(jnp.float32)
+        for e in range(1, edges):
+            drecv = drecv + dpre[e * points : (e + 1) * points].astype(jnp.float32)
+        drecv = drecv.astype(jnp.bfloat16)
+        dreceiver[m] = drecv
+        grad_grid_ref[m] = (dupdated + mxu(drecv, w_recv_ref[...], NT)).astype(jnp.bfloat16)
+        dslot[m] = mxu(pick[...], dpre).astype(jnp.bfloat16)
+        return gain_total
+
+    gain_total = lax.fori_loop(0, members, backward, jnp.zeros((1, width), jnp.float32))
+
+    def put(start, value):
+        value = value.astype(jnp.bfloat16)
+        rows = slice(start, start + value.shape[0])
+        sums_ref[0, rows, :] = value[:, :half]
+        sums_ref[1, rows, :] = value[:, half:]
+
+    def total_of(left, right, lead):
+        edge_total[...] = jnp.zeros_like(edge_total)
+
+        @pl.loop(0, members // lead)
+        def _(t):
+            block = pl.ds(t * lead, lead)
+            rows = lead * left.shape[1]
+            edge_total[...] += mxu(
+                left[block].reshape(rows, width), right[block].reshape(rows, width), TN
+            )
+
+        return edge_total[...]
+
+    put(0, total_of(table_ref, dslot, group))
+    put(width, total_of(grid_ref, dreceiver, 2))
+    put(2 * width, total_of(hidden, dedge, 1))
+    put(
+        3 * width,
+        mxu(
+            dforecast[...].reshape(members * points, lanes),
+            updated[...].reshape(members * points, width),
+            TN,
+        ),
+    )
+    start = 3 * width + lanes
+    tail = sums_ref.shape[1] - start
+    first = lax.broadcasted_iota(jnp.int32, (tail, width), 0) == 0
+    put(start, jnp.where(first, jnp.broadcast_to(gain_total, (tail, width)), 0.0))
+
+    @pl.loop(0, members // group)
+    def _(t):
+        block = pl.ds(t * group, group)
+        back = mxu(dslot[block].reshape(group * slots, width), w_send_ref[...], NT)
+        back = back.reshape(group, slots, width)
+        own_ref[block] = back[:, :own_rows]
+        away_ref[block] = back[:, own_rows:].astype(jnp.bfloat16)
+
+
+def local_pass(
+    grid_latent, table, edge_slot, lat_weight, weight_parts, target, w_send, w_recv, w_edge, gain, head, own_rows, n
+):
+    members, points, width = grid_latent.shape
+    slots = table.shape[1]
+    edges = edge_slot.shape[0]
+    channels = head.shape[1]
+    lanes = -(-channels // 128) * 128
+    rows = 3 * width + lanes + 16
+    rows = -(-rows // (16 * n)) * 16 * n
+    lane_pad = ((0, 0), (0, lanes - channels))
+    stacked = edges * points
+    f32, bf16 = jnp.float32, jnp.bfloat16
+    return pl.pallas_call(
+        functools.partial(local_kernel, channels, points * n),
+        out_shape=(
+            jax.ShapeDtypeStruct(grid_latent.shape, bf16),
+            jax.ShapeDtypeStruct((members, own_rows, width), f32),
+            jax.ShapeDtypeStruct((members, slots - own_rows, width), bf16),
+            jax.ShapeDtypeStruct((2, rows, width // 2), bf16),
+            jax.ShapeDtypeStruct((8, 128), f32),
+        ),
+        in_specs=[pl.BlockSpec(memory_space=pltpu.VMEM)] * 11,
+        out_specs=[pl.BlockSpec(memory_space=pltpu.VMEM)] * 5,
+        scratch_shapes=[
+            pltpu.VMEM((members, slots, width), bf16),
+            pltpu.VMEM((members, stacked, width), f32),
+            pltpu.VMEM((members, stacked, width), f32),
+            pltpu.VMEM((members, stacked, 1), f32),
+            pltpu.VMEM((members, stacked, width), bf16),
+            pltpu.VMEM((members, points, width), bf16),
+            pltpu.VMEM((members, points, lanes), f32),
+            pltpu.VMEM((members, points, lanes), bf16),
+            pltpu.VMEM((members, stacked, width), bf16),
+            pltpu.VMEM((members, points, width), bf16),
+            pltpu.VMEM((members, slots, width), bf16),
+            pltpu.VMEM((slots, stacked), bf16),
+            pltpu.VMEM((width, width), f32),
+        ],
+        compiler_params=pltpu.CompilerParams(vmem_limit_bytes=VMEM_LIMIT),
+    )(
+        grid_latent,
+        table,
+        edge_slot,
+        jnp.broadcast_to(lat_weight[:, None], (points, lanes)),
+        weight_parts,
+        jnp.pad(target.T, lane_pad),
+        w_send,
+        w_recv,
+        w_edge,
+        gain[None],
+        jnp.pad(head, lane_pad),
+    )
+
+
 def corner(value):
     return jnp.broadcast_to(value.reshape(1, 1), (8, 128)).astype(jnp.float32)
-
-
-def split_columns(parts, n):
-    rows = sum(part.shape[0] for part in parts)
-    total = -(-rows // (16 * n)) * 16 * n
-    width = parts[0].shape[1]
-    parts = parts + [jnp.zeros((total - rows, width), jnp.float32)]
-    stacked = jnp.concatenate([part.astype(jnp.bfloat16) for part in parts], axis=0)
-    half = width // 2
-    return jnp.stack([stacked[:, :half], stacked[:, half:]])
 
 
 def body(
@@ -261,7 +486,6 @@
     head_matrix,
 ):
     member_outputs = grid_latent.shape[0]
-    points = grid_latent.shape[1]
     own_rows = mesh_latent.shape[1]
     peer_count = lax.axis_size("space")
     outgoing = send_rows.reshape(-1)
@@ -275,118 +499,48 @@
         arrived.reshape(peer_count, member_outputs, cap, -1), (1, 0, 2, 3)
     ).reshape(member_outputs, peer_count * cap, -1)
     gathered = jnp.concatenate([mesh_latent, arrived], axis=1)
-    lookup = project(gathered, w_send)
-    receiver = jnp.einsum("mgl,lh->mgh", grid_latent, w_recv, preferred_element_type=jnp.float32)
-    pre_acts = []
-    hidden_acts = []
-    normed_list = []
-    inv_stds = []
-    summed = jnp.zeros(grid_latent.shape, jnp.float32)
-    for edge_index in range(edge_slot.shape[0]):
-        pre_act = jnp.take(lookup, edge_slot[edge_index], axis=1).astype(jnp.float32) + receiver
-        hidden_act = jax.nn.silu(pre_act).astype(jnp.bfloat16)
-        edge_out = jnp.einsum("mgh,hl->mgl", hidden_act, w_edge, preferred_element_type=jnp.float32)
-        centred = edge_out - jnp.mean(edge_out, axis=-1, keepdims=True)
-        inv_std = lax.rsqrt(jnp.mean(centred * centred, axis=-1, keepdims=True) + NORM_EPS)
-        normed = centred * inv_std
-        summed = summed + normed * edge_gain
-        pre_acts.append(pre_act)
-        hidden_acts.append(hidden_act)
-        normed_list.append(normed)
-        inv_stds.append(inv_std)
-    refreshed_latent = (grid_latent.astype(jnp.float32) + summed).astype(jnp.bfloat16)
-    prognosis_values = jnp.einsum(
-        "ozw,wd->odz", refreshed_latent, head_matrix, preferred_element_type=jnp.float32
-    )
-    accuracy_term = jnp.mean(softened_absolute(prognosis_values - verifying_analyses[None]), axis=0)
-    member_spread = jnp.sum(
-        softened_absolute(prognosis_values[:, None] - prognosis_values[None, :]), axis=(0, 1)
-    ) / (2.0 * member_outputs * (member_outputs - 1))
-    crps_value = accuracy_term - member_spread
-    weighted = jnp.sum(lat_weight * jnp.sum(crps_value, axis=0))
-    dispersion_factor = lat_weight * (points * peer_count / weight_sum)
-    couple_derivative = jnp.sum(
-        smooth_sign_function(prognosis_values[:, None] - prognosis_values[None, :]), axis=1
-    ) / (member_outputs - 1)
-    prognosis_sensitivity = (
-        dispersion_factor
-        * (smooth_sign_function(prognosis_values - verifying_analyses[None]) - couple_derivative)
-    ).astype(jnp.bfloat16)
-    head_matrix_sensitivity = jnp.einsum(
-        "wru,wuj->rj", prognosis_sensitivity, refreshed_latent, preferred_element_type=jnp.float32
-    )
-    refreshed_latent_adjoint = jnp.einsum(
-        "ord,ur->odu", prognosis_sensitivity, head_matrix, preferred_element_type=jnp.float32
-    )
-    scaled_grad = refreshed_latent_adjoint * edge_gain
-    grad_gain = jnp.zeros(edge_gain.shape, jnp.float32)
-    grad_edge = jnp.zeros(w_edge.shape, jnp.float32)
-    dreceiver = jnp.zeros(receiver.shape, jnp.float32)
-    dpre_list = []
-    for edge_index in range(edge_slot.shape[0]):
-        normed = normed_list[edge_index]
-        grad_gain = grad_gain + jnp.sum(refreshed_latent_adjoint * normed, axis=(0, 1))
-        dedge = inv_stds[edge_index] * (
-            scaled_grad
-            - jnp.mean(scaled_grad, axis=-1, keepdims=True)
-            - normed * jnp.mean(scaled_grad * normed, axis=-1, keepdims=True)
-        )
-        dedge = dedge.astype(jnp.bfloat16)
-        grad_edge = grad_edge + jnp.einsum(
-            "mgh,mgl->hl", hidden_acts[edge_index], dedge, preferred_element_type=jnp.float32
-        )
-        dhidden = jnp.einsum("mgl,hl->mgh", dedge, w_edge, preferred_element_type=jnp.float32)
-        dpre = (dhidden * silu_slope(pre_acts[edge_index])).astype(jnp.bfloat16)
-        dreceiver = dreceiver + dpre.astype(jnp.float32)
-        dpre_list.append(dpre)
-    dreceiver = dreceiver.astype(jnp.bfloat16)
-    grad_grid = (
-        refreshed_latent_adjoint
-        + jnp.einsum("mgh,lh->mgl", dreceiver, w_recv, preferred_element_type=jnp.float32)
-    ).astype(jnp.bfloat16)
-    grad_recv = jnp.einsum(
-        "mgl,mgh->lh", grid_latent, dreceiver, preferred_element_type=jnp.float32
-    )
-    flat_slots = edge_slot.reshape(-1)
-    onehot = (flat_slots[None, :] == jnp.arange(lookup.shape[1], dtype=jnp.int32)[:, None]).astype(
-        jnp.bfloat16
-    )
-    dslot = jnp.einsum(
-        "ts,msh->mth",
-        onehot,
-        jnp.concatenate(dpre_list, axis=1),
-        preferred_element_type=jnp.float32,
-    ).astype(jnp.bfloat16)
-    grad_send = jnp.einsum("mtl,mth->lh", gathered, dslot, preferred_element_type=jnp.float32)
-    grad_lat = jnp.einsum("mth,lh->mtl", dslot, w_send, preferred_element_type=jnp.float32)
+    grad_grid, own_grad, away_grad, sums, weighted = local_pass(
+        grid_latent,
+        gathered,
+        edge_slot,
+        lat_weight,
+        weight_parts,
+        verifying_analyses,
+        w_send,
+        w_recv,
+        w_edge,
+        edge_gain,
+        head_matrix,
+        own_rows,
+        peer_count,
+    )
     slots = jnp.transpose(
-        grad_lat[:, own_rows:].astype(jnp.bfloat16).reshape(member_outputs, peer_count, cap, -1),
-        (1, 0, 2, 3),
+        away_grad.reshape(member_outputs, peer_count, cap, -1), (1, 0, 2, 3)
     ).reshape(peer_count, member_outputs * cap, -1)
-    parts = [grad_send, grad_recv, grad_edge, grad_gain[None], head_matrix_sensitivity]
-    sums, returned, losses = sum_over_space(
-        split_columns(parts, peer_count), slots, corner(weighted), peer_count
-    )
+    sums, returned, losses = sum_over_space(sums, slots, weighted, peer_count)
     returned = jnp.transpose(
         returned.reshape(peer_count, member_outputs, cap, -1), (1, 0, 2, 3)
     ).reshape(member_outputs, peer_count * cap, -1)
-    grad_mesh = grad_lat[:, :own_rows] + fold_rows(returned.astype(jnp.float32), outgoing, own_rows)
-    sums = jnp.concatenate([sums[0], sums[1]], axis=1).astype(jnp.float32)
-    totals = []
-    start = 0
-    for part in parts:
-        totals.append(sums[start : start + part.shape[0]])
-        start += part.shape[0]
+    grad_mesh = own_grad + fold_rows(returned.astype(jnp.float32), outgoing, own_rows)
+    width = w_send.shape[0]
+    channels = head_matrix.shape[1]
+    after = 3 * width + -(-channels // 128) * 128
+
+    def whole(start, count):
+        return jnp.concatenate(
+            [sums[0, start : start + count], sums[1, start : start + count]], axis=1
+        ).astype(jnp.float32)
+
     loss_value = (jnp.sum(losses[:, 0, 0]) / weight_sum).reshape(1)
     return (
         loss_value,
         grad_grid,
         grad_mesh.astype(jnp.bfloat16),
-        totals[0],
-        totals[1],
-        totals[2],
-        totals[3][0],
-        totals[4].T,
+        whole(0, width),
+        whole(width, width),
+        whole(2 * width, width),
+        whole(after, 1)[0],
+        whole(3 * width, channels).T,
     )
 
 

time: 133 us -> 104 us (0.78)
  matrix products: 31.5 us -> 0.92 us
  Pallas kernels: 58.8 us -> 85.4 us
  local copies, waits for them, and re-layouts: 20.6 us -> 7.54 us
  other arithmetic: 17 us -> 6.07 us
    dot_general x19 -> x0, matrix products: 29.5 us -> none  [the longest x1 5.33 us: body(): jnp.einsum('mgl,lh->mgh', grid_latent, w_recv, preferred_element_type=jnp...]
    pallas_call x0 -> x1, Pallas kernels: none -> 26.6 us  [local_pass(): pl.pallas_call(functools.partial(local_kernel, channels, points * n), out...]
    reduce_sum x8 -> x0, other arithmetic: 6.5 us -> none  [the longest x1 2.36 us: body(): jnp.sum(softened_absolute(prognosis_values[:, None] - prognosis_values[No...]
    concatenate x2 -> x0, local copies, waits for them, and re-layouts: 4.64 us -> none  [the longest x1 4.62 us: split_columns(): jnp.concatenate([part.astype(jnp.bfloat16) for part in parts], axis=0)]
    gather x3 -> x0, local copies, waits for them, and re-layouts: 3.87 us -> none  [body(): jnp.take(lookup, edge_slot[edge_index], axis=1).astype(jnp.float32)]
    unnamed x106 -> x23, local copies, waits for them, and re-layouts: 6.26 us -> 3.71 us
    slice x2 -> x1, local copies, waits for them, and re-layouts: 1.76 us -> 0.02 us  [whole(): sums[0, start:start + count]]
    another operation x1 -> x0, other arithmetic: 1.41 us -> none  [split_columns(): return jnp.stack([stacked[:, :half], stacked[:, half:]])]
where the time goes in v2:
time: 104 us; the launch traced here: 103 us
  Pallas kernels  85.4 us (82%)
  local copies, waits for them, and re-layouts  7.54 us (7%)
  other arithmetic  6.07 us (6%)
  between operations  3.33 us (3%)
    pallas_call x1, Pallas kernels, sum_over_space(): pl.pallas_call(functools.partial(sum_kernel, n), out_shape=(jax.ShapeDtyp...  46.4 us
    pallas_call x1, Pallas kernels, local_pass(): pl.pallas_call(functools.partial(local_kernel, channels, points * n), out...  26.6 us
    pallas_call x1, Pallas kernels, exchange_rows(): pl.pallas_call(functools.partial(rows_kernel, n), out_shape=(jax.ShapeDty...  12.4 us
    unnamed x23, local copies, waits for them, and re-layouts  3.71 us
    convert_element_type x3, other arithmetic, whole(): return jnp.concatenate([sums[0, start:start + count], sums[1, start:start...  3.29 us

profile of v2, /device:TPU:0, one launch (start us, length us, event | category | flops | bytes accessed | tf_op | source)
XLA Modules:
  0.0 103.3 jit_solution(12984444057855426146)
XLA Ops:
  0.7 1.3 %fusion.5 = (f32[]{:T(128)}, f32[128]{0:T(128)S(1)}) fusion(s32[128]{0:T(128)} %param.15), kind=kLoop, calls=%fused_computation.29 | loop fusion | flops 767 | bytes 1028 | tf_op jit(solution)/shard_map/reduce_sum | solution.py:495
  2.0 0.6 broadcast_in_dim.6.weight_ref
  2.7 0.8 copy.26
  3.4 0.8 copy.33
  4.5 0.9 copy.29
  5.4 1.1 %copy.30 = bf16[512,83]{1,0:T(8,128)(2,1)S(1)} copy(bf16[512,83]{0,1:T(8,128)(2,1)} %param.21) | data formatting | bytes 169984 | tf_op args[10]
  6.6 0.9 copy-done
  7.5 12.4 %shard_map.170 = (bf16[16,16,512]{2,1,0:T(8,128)(2,1)S(1)}, f32[16,8,128]{2,1,0:T(8,128)S(1)}) custom-call(s32[256,1]{1,0:T(8,128)S(1)} %add.43.sel_ref, bf16[256,512]{1,0:T(8,128)(2,1)S(1)} %bitcast.40, f32[8,128]{1,0:T(8,128)S(1)} %broadcast_in_dim.6.weight_ref), custom_call_target="tpu_custom_call" | custom-call | tf_op jit(solution)/shard_map/pallas_call | solution.py:90
  19.9 0.1 reshape.88
  20.0 0.2 copy.37
  20.2 0.1 reshape.89
  20.4 26.6 %shard_map.171 = (bf16[8,128,512]{2,1,0:T(8,128)(2,1)}, f32[8,32,512]{2,1,0:T(8,128)S(1)}, bf16[8,32,512]{2,1,0:T(8,128)(2,1)S(1)}, bf16[2,1792,256]{2,1,0:T(8,128)(2,1)}, f32[8,128]{1,0:T(8,128)S(1)}) custom-call(bf16[8,128,512]{2,1,0:T(8,128)(2,1)} %grid_ref.1, bf16[8,64,512]{2,1,0:T(8,128)(2,1)S(1)} %pad_maximum_fusion.table_ref, s32[3,128]{1,0:T(4,128)S(1)} %copy-done.5, ...), custom_call_target="tpu_custom_call" | custom-call | tf_op jit(solution)/shard_map/pallas_call | solution.py:429
  47.2 0.2 copy.36
  47.4 0.1 reshape.91.slot_ref
  47.5 46.4 %shard_map.172 = (bf16[2,1792,256]{2,1,0:T(8,128)(2,1)S(1)}, bf16[16,16,512]{2,1,0:T(8,128)(2,1)S(1)}, f32[16,8,128]{2,1,0:T(8,128)S(1)}) custom-call(bf16[2,1792,256]{2,1,0:T(8,128)(2,1)} %get-tuple-element.20.x_ref, bf16[16,16,512]{2,1,0:T(8,128)(2,1)S(1)} %reshape.91.slot_ref, f32[8,128]{1,0:T(8,128)S(1)} %get-tuple-element.22.loss_ref), custom_call_target="tpu_custom_call" | custom-call | tf_op jit(solution)/shard_map/pallas_call | solution.py:195
  93.9 0.6 slice_reduce_fusion
  95.9 0.6 maximum_convert_fusion.3
  96.5 0.9 slice_bitcast_fusion.1
  97.4 0.7 convert_bitcast_fusion
  98.2 0.2 copy.32
  98.4 0.1 reshape.94
  98.5 0.9 fusion.1
  99.4 1.1 %maximum_convert_fusion.2 = f32[512,512]{1,0:T(8,128)} fusion(bf16[512,256]{1,0:T(8,128)(2,1)S(1)} %copy-done.9, bf16[512,256]{1,0:T(8,128)(2,1)S(1)} %copy-done.8), kind=kLoop, calls=%fused_computation.6 | loop fusion | flops 1048576 | bytes 1572864 | tf_op jit(solution)/shard_map/convert_element_type | solution.py:532
  100.6 1.6 %maximum_convert_fusion = (f32[512,512]{1,0:T(8,128)}, f32[512,512]{1,0:T(8,128)}) fusion(bf16[512,256]{1,0:T(8,128)(2,1)S(1)} %get-tuple-element.38, bf16[512,256]{1,0:T(8,128)(2,1)S(1)} %copy-done.7, bf16[512,256]{1,0:T(8,128)(2,1)S(1)} %get-tuple-element.36, bf16[512,256]{1,0:T(8,128)(2,1)S(1)} %get-tuple-element.37), kind=kLoop, calls=%fused_computation.4 | loop fusion | flops 2097152 | bytes 3145728 | tf_op jit(solution)/shard_map/convert_element_type | solution.py:532
  (31 shorter events, 0.7 us)
Async XLA Ops:
  0.6 19.7 %copy-start.1 = (bf16[8,32,512]{2,1,0:T(8,128)(2,1)S(1)}, bf16[8,32,512]{2,1,0:T(8,128)(2,1)}, u32[]{:S(2)}) copy-start(bf16[8,32,512]{2,1,0:T(8,128)(2,1)} %param.12) | copy-start | bytes 786436
  5.4 15.0 %copy-start.2 = (bf16[512,512]{1,0:T(8,128)(2,1)S(1)}, bf16[512,512]{1,0:T(8,128)(2,1)}, u32[]{:S(2)}) copy-start(bf16[512,512]{1,0:T(8,128)(2,1)} %w_send_ref.1) | copy-start | bytes 1572868
  5.4 15.0 %copy-start.5 = (s32[3,128]{1,0:T(4,128)S(1)}, s32[3,128]{1,0:T(4,128)}, u32[]{:S(2)}) copy-start(s32[3,128]{1,0:T(4,128)} %slot_ref.1) | copy-start | bytes 4612
  5.4 15.0 %copy-start.6 = (f32[512]{0:T(512)S(1)}, f32[512]{0:T(512)}, u32[]{:S(2)}) copy-start(f32[512]{0:T(512)} %param.20) | copy-start | bytes 6148
  6.6 1.0 copy-start
  7.5 12.9 %copy-start.3 = (bf16[512,512]{1,0:T(8,128)(2,1)S(1)}, bf16[512,512]{1,0:T(8,128)(2,1)}, u32[]{:S(2)}) copy-start(bf16[512,512]{1,0:T(8,128)(2,1)} %w_recv_ref.1) | copy-start | bytes 1572868
  7.5 12.9 %copy-start.4 = (bf16[512,512]{1,0:T(8,128)(2,1)S(1)}, bf16[512,512]{1,0:T(8,128)(2,1)}, u32[]{:S(2)}) copy-start(bf16[512,512]{1,0:T(8,128)(2,1)} %w_edge_ref.1) | copy-start | bytes 1572868
  97.4 2.0 %copy-start.8 = (bf16[512,256]{1,0:T(8,128)(2,1)S(1)}, bf16[512,256]{1,0:T(8,128)(2,1)}, u32[]{:S(2)}) copy-start(bf16[512,256]{1,0:T(8,128)(2,1)} %get-tuple-element.34) | copy-start | bytes 786436
  97.4 2.0 %copy-start.9 = (bf16[512,256]{1,0:T(8,128)(2,1)S(1)}, bf16[512,256]{1,0:T(8,128)(2,1)}, u32[]{:S(2)}) copy-start(bf16[512,256]{1,0:T(8,128)(2,1)} %get-tuple-element.35) | copy-start | bytes 786436
  98.2 2.3 %copy-start.7 = (bf16[512,256]{1,0:T(8,128)(2,1)S(1)}, bf16[512,256]{1,0:T(8,128)(2,1)}, u32[]{:S(2)}) copy-start(bf16[512,256]{1,0:T(8,128)(2,1)} %get-tuple-element.39) | copy-start | bytes 786436

commit v3 on v2

--- a/solution.py
+++ b/solution.py
@@ -12,20 +12,18 @@
 
 DELTA_SQ = 0.0025
 NORM_EPS = 1e-05
-PRECISE = lax.Precision.HIGHEST
-
-
-def fold_rows(returned, row_ids, row_count):
-    onehot = (row_ids[None, :] == jnp.arange(row_count, dtype=jnp.int32)[:, None]).astype(
-        returned.dtype
-    )
-    return jnp.einsum(
-        "rs,msx->mrx", onehot, returned, preferred_element_type=jnp.float32, precision=PRECISE
-    )
 
 
 MESH_ID = pl.DeviceIdType.MESH
 VMEM_LIMIT = 50 * 1024 * 1024
+
+
+TN = (((0,), (0,)), ((), ()))
+NT = (((1,), (1,)), ((), ()))
+
+
+def mxu(left, right, dims=(((1,), (0,)), ((), ()))):
+    return lax.dot_general(left, right, dims, preferred_element_type=jnp.float32)
 
 
 def greet_all(me, n):
@@ -82,11 +80,15 @@
     swap_rows.wait()
 
 
-def exchange_rows(mesh_latent, send_rows, weight_part, n):
-    members, own_rows, width = mesh_latent.shape
+def sent_rows(send_rows, members, own_rows, n):
     cap = send_rows.shape[-1]
     rows = send_rows.reshape(n, 1, cap) + own_rows * jnp.arange(members, dtype=jnp.int32)[None, :, None]
-    slots = members * cap
+    return rows.reshape(n * members * cap, 1)
+
+
+def exchange_rows(mesh_latent, rows, weight_part, n):
+    members, own_rows, width = mesh_latent.shape
+    slots = rows.shape[0] // n
     return pl.pallas_call(
         functools.partial(rows_kernel, n),
         out_shape=(
@@ -102,16 +104,34 @@
         compiler_params=pltpu.CompilerParams(
             collective_id=0, has_side_effects=True, vmem_limit_bytes=VMEM_LIMIT
         ),
-    )(rows.reshape(n * slots, 1), mesh_latent.reshape(members * own_rows, width), weight_part)
+    )(rows, mesh_latent.reshape(members * own_rows, width), weight_part)
+
+
+STREAMS = 4
+TOGETHER = 2
 
 
 def stream_bits(n):
     bits = [1 << k for k in range(n.bit_length() - 1)]
-    return [bits, bits[:1] + bits[2:] + bits[1:2]]
+    return [bits, bits[:1] + bits[2:] + bits[1:2]] * (STREAMS // 2)
 
 
 def sum_kernel(
-    n, x_ref, slot_ref, loss_ref, out_ref, ret_ref, losses_ref, work, landed, send_sems, recv_sems, sems
+    n,
+    x_ref,
+    slot_ref,
+    loss_ref,
+    sel_ref,
+    own_ref,
+    out_ref,
+    mesh_ref,
+    losses_ref,
+    work,
+    landed,
+    ret_ref,
+    send_sems,
+    recv_sems,
+    sems,
 ):
     me = lax.axis_index("space")
     greet_all(me, n)
@@ -175,51 +195,50 @@
     swap_losses = swap_blocks(me, n, loss_ref, losses_ref, sems.at[2], sems.at[3], False)
     ret_ref[me] = slot_ref[me]
     losses_ref[me] = loss_ref[...]
-    for k in range(steps):
+    for k in range(2 * steps):
         for s in range(len(streams)):
             copies[s].wait()
-            add(s, k)
-            copies[s] = halve(s, k + 1) if k < steps - 1 else spread(s, k)
-    for k in reversed(range(steps)):
-        for s in range(len(streams)):
-            copies[s].wait()
-            if k > 0:
-                copies[s] = spread(s, k - 1)
-    swap_slots.wait()
+            if k < steps:
+                add(s, k)
+            if k < steps - 1:
+                copies[s] = halve(s, k + 1)
+            elif k < 2 * steps - 1:
+                copies[s] = spread(s, 2 * steps - 2 - k)
+        if k == steps - 1:
+            swap_slots.wait()
+            members, own_rows, width = own_ref.shape
+            sel = sel_ref[...]
+            pick = (
+                sel == lax.broadcasted_iota(jnp.int32, (sel.shape[0], members * own_rows), 1)
+            ).astype(jnp.bfloat16)
+            back = mxu(pick, ret_ref[...].reshape(sel.shape[0], width), TN)
+            mesh_ref[...] = (own_ref[...] + back.reshape(own_ref.shape)).astype(jnp.bfloat16)
     swap_losses.wait()
 
 
-def sum_over_space(x, slots, loss, n):
-    streams = len(stream_bits(n))
+def sum_over_space(x, slots, loss, rows, own, n):
     steps = n.bit_length() - 1
     return pl.pallas_call(
         functools.partial(sum_kernel, n),
         out_shape=(
             jax.ShapeDtypeStruct(x.shape, x.dtype),
-            jax.ShapeDtypeStruct(slots.shape, slots.dtype),
+            jax.ShapeDtypeStruct(own.shape, slots.dtype),
             jax.ShapeDtypeStruct((n,) + loss.shape, loss.dtype),
         ),
-        in_specs=[pl.BlockSpec(memory_space=pltpu.VMEM)] * 3,
+        in_specs=[pl.BlockSpec(memory_space=pltpu.VMEM)] * 5,
         out_specs=[pl.BlockSpec(memory_space=pltpu.VMEM)] * 3,
         scratch_shapes=[
             pltpu.VMEM(x.shape, x.dtype),
             pltpu.VMEM(x.shape, x.dtype),
-            pltpu.SemaphoreType.DMA((streams, 2 * steps)),
-            pltpu.SemaphoreType.DMA((streams, 2 * steps)),
+            pltpu.VMEM(slots.shape, slots.dtype),
+            pltpu.SemaphoreType.DMA((STREAMS, 2 * steps)),
+            pltpu.SemaphoreType.DMA((STREAMS, 2 * steps)),
             pltpu.SemaphoreType.DMA((4,)),
         ],
         compiler_params=pltpu.CompilerParams(
             collective_id=1, has_side_effects=True, vmem_limit_bytes=VMEM_LIMIT
         ),
-    )(x, slots, loss)
-
-
-TN = (((0,), (0,)), ((), ()))
-NT = (((1,), (1,)), ((), ()))
-
-
-def mxu(left, right, dims=(((1,), (0,)), ((), ()))):
-    return lax.dot_general(left, right, dims, preferred_element_type=jnp.float32)
+    )(x, slots, loss, rows, own)
 
 
 def local_kernel(
@@ -254,13 +273,14 @@
     dslot,
     pick,
     edge_total,
+    truth,
 ):
     members, points, width = grid_ref.shape
     slots = table_ref.shape[1]
     own_rows = own_ref.shape[1]
     edges = slot_ref.shape[0]
     gain = gain_ref[...]
-    half = width // 2
+    part = sums_ref.shape[2]
 
     for e in range(edges):
         row = slot_ref[pl.ds(e, 1), :]
@@ -278,8 +298,7 @@
         sent = mxu(rows, w_send_ref[...]).astype(jnp.bfloat16)
         sender[pl.ds(t * group, group)] = sent.reshape(group, slots, width)
 
-    @pl.loop(0, members)
-    def _(m):
+    def forward(m):
         latent = grid_ref[m]
         receiver = mxu(latent, w_recv_ref[...])
         v = mxu(pick[...], sender[m], TN) + jnp.concatenate([receiver] * edges, axis=0)
@@ -299,8 +318,14 @@
             summed = summed + scaled[e * points : (e + 1) * points]
         fresh = (latent.astype(jnp.float32) + summed * gain).astype(jnp.bfloat16)
         updated[m] = fresh
-        forecast[m] = mxu(fresh, head_ref[...])
-
+        forecast[m] = mxu(fresh, head_ref[...], NT)
+
+    @pl.loop(0, members // TOGETHER)
+    def _(t):
+        for u in range(TOGETHER):
+            forward(t * TOGETHER + u)
+
+    truth[...] = target_ref[...].T
     weight_sum = jnp.sum(weights_ref[...], axis=0)[:1, :]
     factor_scale = grid_total / weight_sum
     chunk = 16
@@ -310,7 +335,7 @@
     def score(t, total):
         rows = pl.ds(pl.multiple_of(t * chunk, chunk), chunk)
         weight = lat_ref[rows, :]
-        target = target_ref[rows, :]
+        target = truth[rows, :]
         values = [forecast[m, rows, :] for m in range(members)]
         accuracy = jnp.zeros((chunk, lanes), jnp.float32)
         spread = jnp.zeros((chunk, lanes), jnp.float32)
@@ -345,7 +370,7 @@
     loss_ref[...] = jnp.broadcast_to(total, loss_ref.shape)
 
     def backward(m, gain_total):
-        dupdated = mxu(dforecast[m], head_ref[...], NT)
+        dupdated = mxu(dforecast[m], head_ref[...])
         scaled_grad = dupdated * gain
         shifted = scaled_grad - jnp.mean(scaled_grad, axis=-1, keepdims=True)
         norm_sum = jnp.zeros((points, width), jnp.float32)
@@ -367,13 +392,20 @@
         dslot[m] = mxu(pick[...], dpre).astype(jnp.bfloat16)
         return gain_total
 
-    gain_total = lax.fori_loop(0, members, backward, jnp.zeros((1, width), jnp.float32))
+    def backward_group(t, gain_total):
+        for u in range(TOGETHER):
+            gain_total = backward(t * TOGETHER + u, gain_total)
+        return gain_total
+
+    gain_total = lax.fori_loop(
+        0, members // TOGETHER, backward_group, jnp.zeros((1, width), jnp.float32)
+    )
 
     def put(start, value):
         value = value.astype(jnp.bfloat16)
         rows = slice(start, start + value.shape[0])
-        sums_ref[0, rows, :] = value[:, :half]
-        sums_ref[1, rows, :] = value[:, half:]
+        for s in range(sums_ref.shape[0]):
+            sums_ref[s, rows, :] = value[:, s * part : (s + 1) * part]
 
     def total_of(left, right, lead):
         edge_total[...] = jnp.zeros_like(edge_total)
@@ -423,7 +455,6 @@
     lanes = -(-channels // 128) * 128
     rows = 3 * width + lanes + 16
     rows = -(-rows // (16 * n)) * 16 * n
-    lane_pad = ((0, 0), (0, lanes - channels))
     stacked = edges * points
     f32, bf16 = jnp.float32, jnp.bfloat16
     return pl.pallas_call(
@@ -432,7 +463,7 @@
             jax.ShapeDtypeStruct(grid_latent.shape, bf16),
             jax.ShapeDtypeStruct((members, own_rows, width), f32),
             jax.ShapeDtypeStruct((members, slots - own_rows, width), bf16),
-            jax.ShapeDtypeStruct((2, rows, width // 2), bf16),
+            jax.ShapeDtypeStruct((STREAMS, rows, width // STREAMS), bf16),
             jax.ShapeDtypeStruct((8, 128), f32),
         ),
         in_specs=[pl.BlockSpec(memory_space=pltpu.VMEM)] * 11,
@@ -451,6 +482,7 @@
             pltpu.VMEM((members, slots, width), bf16),
             pltpu.VMEM((slots, stacked), bf16),
             pltpu.VMEM((width, width), f32),
+            pltpu.VMEM((points, lanes), f32),
         ],
         compiler_params=pltpu.CompilerParams(vmem_limit_bytes=VMEM_LIMIT),
     )(
@@ -459,12 +491,12 @@
         edge_slot,
         jnp.broadcast_to(lat_weight[:, None], (points, lanes)),
         weight_parts,
-        jnp.pad(target.T, lane_pad),
+        jnp.pad(target, ((0, lanes - channels), (0, 0))),
         w_send,
         w_recv,
         w_edge,
         gain[None],
-        jnp.pad(head, lane_pad),
+        jnp.pad(head.T, ((0, lanes - channels), (0, 0))),
     )
 
 
@@ -488,11 +520,11 @@
     member_outputs = grid_latent.shape[0]
     own_rows = mesh_latent.shape[1]
     peer_count = lax.axis_size("space")
-    outgoing = send_rows.reshape(-1)
+    rows = sent_rows(send_rows, member_outputs, own_rows, peer_count)
     cap = send_rows.shape[-1]
     lat_weight = jnp.cos(jnp.pi * ((lat_row.astype(jnp.float32) + 0.5) / LATS - 0.5))
     arrived, weight_parts = exchange_rows(
-        mesh_latent, send_rows, corner(jnp.sum(lat_weight)), peer_count
+        mesh_latent, rows, corner(jnp.sum(lat_weight)), peer_count
     )
     weight_sum = jnp.sum(weight_parts[:, 0, 0])
     arrived = jnp.transpose(
@@ -517,25 +549,21 @@
     slots = jnp.transpose(
         away_grad.reshape(member_outputs, peer_count, cap, -1), (1, 0, 2, 3)
     ).reshape(peer_count, member_outputs * cap, -1)
-    sums, returned, losses = sum_over_space(sums, slots, weighted, peer_count)
-    returned = jnp.transpose(
-        returned.reshape(peer_count, member_outputs, cap, -1), (1, 0, 2, 3)
-    ).reshape(member_outputs, peer_count * cap, -1)
-    grad_mesh = own_grad + fold_rows(returned.astype(jnp.float32), outgoing, own_rows)
+    sums, grad_mesh, losses = sum_over_space(sums, slots, weighted, rows, own_grad, peer_count)
     width = w_send.shape[0]
     channels = head_matrix.shape[1]
     after = 3 * width + -(-channels // 128) * 128
 
     def whole(start, count):
         return jnp.concatenate(
-            [sums[0, start : start + count], sums[1, start : start + count]], axis=1
+            [sums[s, start : start + count] for s in range(STREAMS)], axis=1
         ).astype(jnp.float32)
 
     loss_value = (jnp.sum(losses[:, 0, 0]) / weight_sum).reshape(1)
     return (
         loss_value,
         grad_grid,
-        grad_mesh.astype(jnp.bfloat16),
+        grad_mesh,
         whole(0, width),
         whole(width, width),
         whole(2 * width, width),

time: 104 us -> 94.9 us (0.913)
  Pallas kernels: 85.4 us -> 79.5 us
  local copies, waits for them, and re-layouts: 7.54 us -> 5.89 us
    pallas_call x1, Pallas kernels: 46.4 us -> 42.3 us  [sum_over_space(): pl.pallas_call(functools.partial(sum_kernel, n), out_shape=(jax.ShapeDtyp...]
    unnamed x23 -> x15, local copies, waits for them, and re-layouts: 3.71 us -> 1.67 us
    pallas_call x1, Pallas kernels: 26.6 us -> 24.8 us  [local_pass(): pl.pallas_call(functools.partial(local_kernel, channels, points * n), out...]
    pad x2, local copies, waits for them, and re-layouts: 0.04 us -> 1.7 us  [the longest x1 0.9 us: local_pass(): jnp.pad(head.T, ((0, lanes - channels), (0, 0)))]
where the time goes in v3:
time: 94.9 us; the launch traced here: 94.6 us
  Pallas kernels  79.5 us (84%)
  local copies, waits for them, and re-layouts  5.89 us (6%)
  other arithmetic  5.86 us (6%)
  between operations  3.28 us (3%)
    pallas_call x1, Pallas kernels, sum_over_space(): pl.pallas_call(functools.partial(sum_kernel, n), out_shape=(jax.ShapeDtyp...  42.3 us
    pallas_call x1, Pallas kernels, local_pass(): pl.pallas_call(functools.partial(local_kernel, channels, points * n), out...  24.8 us
    pallas_call x1, Pallas kernels, exchange_rows(): pl.pallas_call(functools.partial(rows_kernel, n), out_shape=(jax.ShapeDty...  12.4 us
    convert_element_type x3, other arithmetic, whole(): return jnp.concatenate([sums[s, start:start + count] for s in range(STREA...  3.08 us

profile of v3, /device:TPU:0, one launch (start us, length us, event | category | flops | bytes accessed | tf_op | source)
XLA Modules:
  0.0 94.6 jit_solution(9762879772610267939)
XLA Ops:
  0.7 1.3 %fusion = (f32[]{:T(128)}, f32[128]{0:T(128)S(1)}) fusion(s32[128]{0:T(128)} %param.15), kind=kLoop, calls=%fused_computation.33 | loop fusion | flops 767 | bytes 1028 | tf_op jit(solution)/shard_map/reduce_sum | solution.py:527
  2.0 0.6 broadcast_in_dim.6.weight_ref
  2.7 0.8 copy.22
  3.4 0.1 broadcast_add_fusion
  3.6 0.1 add.39.sel_ref
  3.7 0.8 pad.8.target_ref
  4.5 0.9 pad.9.head_ref
  5.4 0.9 copy-done
  6.3 12.4 %shard_map.170 = (bf16[16,16,512]{2,1,0:T(8,128)(2,1)S(1)}, f32[16,8,128]{2,1,0:T(8,128)S(1)}) custom-call(s32[256,1]{1,0:T(8,128)S(1)} %add.39.sel_ref, bf16[256,512]{1,0:T(8,128)(2,1)S(1)} %bitcast.53, f32[8,128]{1,0:T(8,128)S(1)} %broadcast_in_dim.6.weight_ref), custom_call_target="tpu_custom_call" | custom-call | tf_op jit(solution)/shard_map/pallas_call | solution.py:92
  18.8 0.1 reshape.93
  18.9 0.2 copy.30
  19.1 0.1 reshape.94
  19.3 24.8 %shard_map.171 = (bf16[8,128,512]{2,1,0:T(8,128)(2,1)}, f32[8,32,512]{2,1,0:T(8,128)S(1)}, bf16[8,32,512]{2,1,0:T(8,128)(2,1)S(1)}, bf16[4,1792,128]{2,1,0:T(8,128)(2,1)}, f32[8,128]{1,0:T(8,128)S(1)}) custom-call(bf16[8,128,512]{2,1,0:T(8,128)(2,1)} %grid_ref.1, bf16[8,64,512]{2,1,0:T(8,128)(2,1)S(1)} %pad_maximum_fusion.table_ref, s32[3,128]{1,0:T(4,128)S(1)} %copy-done.5, ...), custom_call_target="tpu_custom_call" | custom-call | tf_op jit(solution)/shard_map/pallas_call | solution.py:460
  44.1 0.1 reshape.95
  44.2 0.2 copy.29
  44.4 0.1 reshape.96.slot_ref
  44.5 42.3 %shard_map.172 = (bf16[4,1792,128]{2,1,0:T(8,128)(2,1)S(1)}, bf16[8,32,512]{2,1,0:T(8,128)(2,1)S(1)}, f32[16,8,128]{2,1,0:T(8,128)S(1)}) custom-call(bf16[4,1792,128]{2,1,0:T(8,128)(2,1)} %get-tuple-element.20.x_ref, bf16[16,16,512]{2,1,0:T(8,128)(2,1)S(1)} %reshape.96.slot_ref, f32[8,128]{1,0:T(8,128)S(1)} %get-tuple-element.22.loss_ref, ...), custom_call_target="tpu_custom_call" | custom-call | tf_op jit(solution)/shard_map/pallas_call | solution.py:221
  86.9 0.6 slice_reduce_fusion
  88.8 0.6 maximum_convert_fusion.3
  89.4 0.1 slice_bitcast_fusion.3
  89.6 0.7 convert_bitcast_fusion
  90.2 1.0 %maximum_convert_fusion.2 = f32[512,512]{1,0:T(8,128)} fusion(bf16[512,128]{1,0:T(8,128)(2,1)S(1)} %get-tuple-element.39, bf16[512,128]{1,0:T(8,128)(2,1)S(1)} %get-tuple-element.40, bf16[512,128]{1,0:T(8,128)(2,1)S(1)} %get-tuple-element.41, bf16[512,128]{1,0:T(8,128)(2,1)S(1)} %get-tuple-element.38), kind=kLoop, calls=%fused_computation.3 | loop fusion | flops 2097152 | bytes 1572864 | tf_op jit(solution)/shard_map/convert_element_type | solution.py:560
  91.3 1.5 %maximum_convert_fusion = (f32[512,512]{1,0:T(8,128)}, f32[512,512]{1,0:T(8,128)}) fusion(bf16[512,128]{1,0:T(8,128)(2,1)S(1)} %get-tuple-element.46, bf16[512,128]{1,0:T(8,128)(2,1)S(1)} %get-tuple-element.47, bf16[512,128]{1,0:T(8,128)(2,1)S(1)} %get-tuple-element.48, bf16[512,128]{1,0:T(8,128)(2,1)S(1)} %get-tuple-element.49, ...), kind=kLoop, calls=%fused_computation.1 | loop fusion | flops 4194304 | bytes 3145728 | tf_op jit(solution)/shard_map/convert_element_type | solution.py:560
  92.7 0.7 copy.32
  (18 shorter events, 0.2 us)
Async XLA Ops:
  0.6 18.6 %copy-start.1 = (bf16[8,32,512]{2,1,0:T(8,128)(2,1)S(1)}, bf16[8,32,512]{2,1,0:T(8,128)(2,1)}, u32[]{:S(2)}) copy-start(bf16[8,32,512]{2,1,0:T(8,128)(2,1)} %param.12) | copy-start | bytes 786436
  3.4 15.8 %copy-start.5 = (s32[3,128]{1,0:T(4,128)S(1)}, s32[3,128]{1,0:T(4,128)}, u32[]{:S(2)}) copy-start(s32[3,128]{1,0:T(4,128)} %slot_ref.1) | copy-start | bytes 4612
  3.4 15.8 %copy-start.6 = (f32[512]{0:T(512)S(1)}, f32[512]{0:T(512)}, u32[]{:S(2)}) copy-start(f32[512]{0:T(512)} %param.20) | copy-start | bytes 6148
  5.4 1.0 %copy-start = (bf16[8,32,512]{2,1,0:T(8,128)(2,1)S(1)}, bf16[8,32,512]{2,1,0:T(8,128)(2,1)}, u32[]{:S(2)}) copy-start(bf16[8,32,512]{2,1,0:T(8,128)(2,1)} %param.12) | copy-start | bytes 786436
  6.3 12.9 %copy-start.2 = (bf16[512,512]{1,0:T(8,128)(2,1)S(1)}, bf16[512,512]{1,0:T(8,128)(2,1)}, u32[]{:S(2)}) copy-start(bf16[512,512]{1,0:T(8,128)(2,1)} %w_send_ref.1) | copy-start | bytes 1572868
  6.3 13.0 %copy-start.3 = (bf16[512,512]{1,0:T(8,128)(2,1)S(1)}, bf16[512,512]{1,0:T(8,128)(2,1)}, u32[]{:S(2)}) copy-start(bf16[512,512]{1,0:T(8,128)(2,1)} %w_recv_ref.1) | copy-start | bytes 1572868
  6.3 13.0 %copy-start.4 = (bf16[512,512]{1,0:T(8,128)(2,1)S(1)}, bf16[512,512]{1,0:T(8,128)(2,1)}, u32[]{:S(2)}) copy-start(bf16[512,512]{1,0:T(8,128)(2,1)} %w_edge_ref.1) | copy-start | bytes 1572868
